TPU v7x, 32 devices: a whole 2x2x4 slice. The times are simulated.
32 devices in a mesh: blk: 16 (over z, x, core), pair: 2 (over y).
Axes of the slice: x: 2, y: 2, z: 4, core: 2. Of those that a mesh axis runs over, the one named last changes fastest.
Arguments:
- tokens_in: bfloat16 [4096, 2560], P(('blk', 'pair')), may hold values from -6 to 6
- cotangent: bfloat16 [4096, 2560], P(('blk', 'pair')), may hold values from -6 to 6
- w_qkv: float32 [2560, 3072], P(('blk', 'pair')), may hold values from -0.125 to 0.125
- w_out: float32 [2560, 2560], P(None, ('blk', 'pair')), may hold values from -3.5 to 3.5
- w_gateup: float32 [2, 2560, 7680], P(None, ('blk', 'pair')), may hold values from -0.125 to 0.125
- w_down: float32 [7680, 2560], P(None, ('blk', 'pair')), may hold values from -0.125 to 0.125
- gains: float32 [2, 2560], P(None, ('blk', 'pair')), may hold values from 0.5 to 1.5
- mom_qkv: float32 [2560, 3072], P(('blk', 'pair')), may hold values from -512 to 512
- mom_out: float32 [2560, 2560], P(None, ('blk', 'pair')), may hold values from -20 to 20
- mom_gateup: float32 [2, 2560, 7680], P(None, ('blk', 'pair')), may hold values from -320 to 320
- mom_down: float32 [7680, 2560], P(None, ('blk', 'pair')), may hold values from -224 to 224
- mom_gains: float32 [2, 2560], P(None, ('blk', 'pair')), may hold values from -768 to 768
Outputs:
- block_output: bfloat16 [4096, 2560], P(('blk', 'pair'))
- input_grad: float32 [4096, 2560], P(('blk', 'pair'))
- new_w_qkv: float32 [2560, 3072], P(('blk', 'pair'))
- moment_qkv: float32 [2560, 3072], P(('blk', 'pair'))
- copy_qkv: bfloat16 [2560, 3072], P(('blk', 'pair'))
- new_w_out: float32 [2560, 2560], P(None, ('blk', 'pair'))
- moment_out: float32 [2560, 2560], P(None, ('blk', 'pair'))
- copy_out: bfloat16 [2560, 2560], P(None, ('blk', 'pair'))
- new_w_gateup: float32 [2, 2560, 7680], P(None, ('blk', 'pair'))
- moment_gateup: float32 [2, 2560, 7680], P(None, ('blk', 'pair'))
- copy_gateup: bfloat16 [2, 2560, 7680], P(None, ('blk', 'pair'))
- new_w_down: float32 [7680, 2560], P(None, ('blk', 'pair'))
- moment_down: float32 [7680, 2560], P(None, ('blk', 'pair'))
- copy_down: bfloat16 [7680, 2560], P(None, ('blk', 'pair'))
- new_gains: float32 [2, 2560], P(None, ('blk', 'pair'))
- moment_gains: float32 [2, 2560], P(None, ('blk', 'pair'))
- copy_gains: bfloat16 [2, 2560], P(None, ('blk', 'pair'))
All inputs are finite; a program needn't handle non-finite values.
Results may differ from a plain program's by a relative error of at most 0.04.
Values may be sent and summed in bfloat16 or wider, within the bound.
A program may use at most 640 MiB of HBM per device.

v0:
```python
import functools
from typing import NamedTuple

import jax
import jax.numpy as jnp
from jax import lax
from jax.experimental import pallas as pl
from jax.experimental.pallas import tpu as pltpu
from jax.sharding import PartitionSpec as P

H = 10
HEAD = 256
FF = 7680
WINDOW = 2048
NS_STEPS = 5


eps_norm = 1e-06
eps_pieces = 1e-07
ns_first = 3.4445
ns_second = -4.775
ns_third = 2.0315
momentum_decay = 0.95
matrix_rate = 0.5
output_rate = 10.0
gain_rate = 0.001
weight_shrink = 0.001
masked_score = -1e30
MESH = pl.DeviceIdType.MESH


def position():
    blk, y = lax.axis_index("blk"), lax.axis_index("pair")
    return blk, lax.div(blk, 4), lax.rem(lax.div(blk, 2), 2), lax.rem(blk, 2), y


def greet(devices):
    barrier = pltpu.get_barrier_semaphore()
    for device in devices:
        pl.semaphore_signal(barrier, inc=1, device_id=device, device_id_type=MESH)
    pl.semaphore_wait(barrier, len(devices))


def remote(source, target, send_sem, recv_sem, device):
    return pltpu.make_async_remote_copy(
        src_ref=source,
        dst_ref=target,
        send_sem=send_sem,
        recv_sem=recv_sem,
        device_id=device,
        device_id_type=MESH,
    )


class Exchange(NamedTuple):
    packets: jax.Array
    among: str
    sources: int
    first_target: int = 0
    spread_sources: bool = False
    spread_targets: bool = False


def spread_place(planes, blk):
    z, x, core = lax.div(blk, 4), lax.rem(lax.div(blk, 2), 2), lax.rem(blk, 2)
    return (2 * core + lax.rem(x + z, 2)) * planes + z


def all_devices():
    blk, _, _, _, y = position()
    count = 2 * lax.axis_size("blk")
    here = 2 * blk + y
    places = [lax.rem(here + at, count) for at in range(1, count)]
    return [(lax.div(place, 2), lax.rem(place, 2)) for place in places]


def plane_devices():
    blk, _, _, _, y = position()
    count = lax.axis_size("blk")
    return [(lax.rem(blk + at, count), y) for at in range(1, count)]


def greeted(specs, nearby):
    if any(among == "all" for among, *_ in specs):
        return all_devices()
    blk, _, _, _, y = position()
    pair = [(blk, 1 - y)] * any(among == "pair" for among, *_ in specs)
    if any(among == "plane" for among, *_ in specs):
        return plane_devices() + pair
    return nearby + pair


PAIR_PARTS = 4


def exchange_count(planes, among):
    return {"all": 8 * planes, "plane": 4 * planes, "pair": PAIR_PARTS}[among]


class Ride:
    def __init__(self, planes, spec, packets, received, sems):
        self.planes, self.packets, self.received = planes, packets, received
        self.among, self.sources, self.first_target, self.from_spread, self.to_spread = spec
        self.own_sem, self.send_sems, self.recv_sems = sems
        self.count = exchange_count(planes, self.among)
        self.issued = 0
        blk, self.z, _, _, self.y = position()
        self.blk = blk
        self.here = blk if self.among == "plane" else 2 * blk + self.y

    def place(self, q):
        near = self.count // self.planes
        spot = lax.rem(self.z + 1 + lax.rem(q, self.planes), self.planes)
        return spot * near + lax.rem(self.here + lax.div(q, self.planes), near)

    def counted(self, place, spread):
        if not spread:
            return place
        if self.among == "plane":
            return spread_place(self.planes, place)
        return 2 * spread_place(self.planes, lax.div(place, 2)) + lax.rem(place, 2)

    def source(self, place):
        return self.counted(place, self.from_spread)

    def target(self, place):
        return self.counted(place, self.to_spread) - self.first_target

    def sending(self, place):
        return self.source(place) < self.sources

    def receiving(self, place):
        target = self.target(place)
        return (target >= 0) & (target < self.packets.shape[0])

    def copy(self, q):
        if self.among == "pair":
            rows = self.packets.shape[0] // PAIR_PARTS
            some = pl.ds(pl.multiple_of(q * rows, rows), rows)
            return remote(
                self.packets.at[some],
                self.received.at[some],
                self.send_sems.at[q],
                self.recv_sems.at[q],
                (self.blk, 1 - self.y),
            )
        place = self.place(q)
        device = (place, self.y)
        if self.among == "all":
            device = (lax.div(place, 2), lax.rem(place, 2))
        source = self.source(self.here)
        return remote(
            self.packets.at[self.target(place)],
            self.received.at[source],
            self.send_sems.at[q],
            self.recv_sems.at[source],
            device,
        )

    def own(self):
        return pltpu.make_async_copy(
            self.packets.at[self.target(self.here)],
            self.received.at[self.source(self.here)],
            self.own_sem.at[0],
        )

    def sends(self, q):
        away = (q < self.count) & (q != self.planes - 1)
        return away & self.sending(self.here) & self.receiving(self.place(q))

    def keeps(self):
        return self.sending(self.here) & self.receiving(self.here)

    def start_own(self):
        if self.among == "pair":
            for q in range(self.count):
                self.copy(q).start()
        else:

            @pl.when(self.keeps())
            def _():
                self.own().start()

    def issue(self, q):
        if self.among != "pair":

            @pl.when(self.sends(q))
            def _():
                self.copy(q).start()

    def issue_more(self, number):
        first, self.issued = self.issued, min(self.issued + number, self.count)

        @pl.loop(first, self.issued)
        def _(q):
            self.issue(q)

    def finish(self):
        if self.among == "pair":
            for q in range(self.count):
                self.copy(q).wait()
            return

        @pl.loop(0, self.count)
        def _(q):
            @pl.when(self.sends(q))
            def _():
                self.copy(q).wait_send()

            @pl.when((q != self.here) & self.sending(q) & self.receiving(self.here))
            def _():
                source = self.source(q)
                spot = self.received.at[source]
                remote(
                    spot, spot, self.own_sem.at[0], self.recv_sems.at[source], (self.blk, self.y)
                ).wait_recv()

        @pl.when(self.keeps())
        def _():
            self.own().wait()


def rides_of(planes, rides):
    rides = [Ride(planes, *ride) for ride in rides]
    for ride in rides:
        ride.start_own()
    return rides


def exchange_sems(exchanges, planes):
    dma = pltpu.SemaphoreType.DMA
    return [
        dma((count,))
        for exchange in exchanges
        for count in (1,) + (exchange_count(planes, exchange.among),) * 2
    ]


def exchange_specs(exchanges):
    return tuple((each.among, *each[2:]) for each in exchanges)


def communicate(
    kernel,
    operands,
    exchanges,
    outputs,
    scratch,
    planes,
    collective_id,
    cost,
    name,
    out_spec=pl.ANY,
    **options,
):
    packets = [each.packets for each in exchanges]
    received = [
        jax.ShapeDtypeStruct(
            array.shape
            if each.among == "pair"
            else (exchange_count(planes, each.among), *array.shape[1:]),
            array.dtype,
        )
        for each, array in zip(exchanges, packets)
    ]
    any_spec = pl.BlockSpec(memory_space=pl.ANY)
    return pl.pallas_call(
        kernel,
        out_shape=outputs + received,
        in_specs=[any_spec] * (len(operands) + len(packets)),
        out_specs=[pl.BlockSpec(memory_space=out_spec)] * len(outputs) + [any_spec] * len(packets),
        scratch_shapes=scratch + exchange_sems(exchanges, planes),
        compiler_params=pltpu.CompilerParams(
            collective_id=collective_id, has_side_effects=True, **options
        ),
        cost_estimate=pl.CostEstimate(flops=0, bytes_accessed=cost * 2**20, transcendentals=0),
        name=name,
    )(*operands, *packets)


def split_refs(refs, inputs, outputs, specs):
    riders = len(specs)
    ins, refs = refs[: inputs + riders], refs[inputs + riders :]
    outs, refs = refs[: outputs + riders], refs[outputs + riders :]
    scratch = refs[: len(refs) - 3 * riders]
    sems = refs[len(refs) - 3 * riders :]
    rides = [
        (spec, ins[inputs + i], outs[outputs + i], sems[3 * i : 3 * i + 3])
        for i, spec in enumerate(specs)
    ]
    return ins[:inputs], outs[:outputs], scratch, rides


def exchange_kernel(planes, specs, *refs):
    _, _, _, rides = split_refs(refs, 0, 0, specs)
    greet(greeted(specs, []))
    rides = rides_of(planes, rides)
    for ride in rides:
        ride.issue_more(ride.count)
    for ride in rides:
        ride.finish()


def exchange_now(exchanges, planes, collective_id):
    specs = exchange_specs(exchanges)
    kernel = functools.partial(exchange_kernel, planes, specs)
    return communicate(kernel, [], exchanges, [], [], planes, collective_id, 100, "exchange_now")


def gather_kernel(planes, parts, whole_slice, specs, *refs):
    arrays = 1 + max(array for array, *_ in parts)
    shard_refs, whole_refs, scratch, rides = split_refs(refs, arrays, arrays, specs)
    count = len(parts)
    shards = [shard_refs[array].at[pl.ds(start, size)] for array, start, size, _ in parts]
    late = [is_late for *_, is_late in parts]
    own_sem, line_send, second_send, first_send, core_send, recv, core_recv = scratch
    blk, z, x, core, y = position()
    firsts = 2 if whole_slice else 1
    to_core = (blk + 1 - 2 * core, y)
    if whole_slice:
        first = y * (1 - core) + x * core
        second = x * (1 - core) + y * core
        first_device = (blk + core * (2 - 4 * x), y + (1 - core) * (1 - 2 * y))
        second_device = (blk + (1 - core) * (2 - 4 * x), y + core * (1 - 2 * y))
    else:
        first, second = 0, x
        first_device, second_device = None, (blk + 2 - 4 * x, y)
    line = [(blk + 4 * (lax.rem(z + at, planes) - z), y) for at in range(1, planes)]
    nearby = [to_core, second_device] + [first_device] * whole_slice + line
    greet(greeted(specs, nearby))

    def slot(i, spot, by_first, by_second, plane):
        array, start, size, _ = parts[i]
        whole, some = whole_refs[array], pl.ds(start, size)
        if whole_slice:
            by_x = (1 - plane) * by_second + plane * by_first
            by_y = (1 - plane) * by_first + plane * by_second
            return whole.at[spot, by_x, plane, by_y, some]
        return whole.at[spot, by_second, plane, some]

    def arrive(i, spot, by_first, by_second):
        here = slot(i, spot, by_first, by_second, core)
        remote(here, here, own_sem.at[0], recv.at[i, spot, by_first, by_second], to_core).wait_recv()

    def along(i, source, spot, turn, way):
        by_second = second if turn == 0 else 1 - second
        target = slot(i, spot, first, by_second, core)
        sems = line_send.at[way, i, spot, turn], recv.at[i, spot, first, by_second]
        return remote(source, target, *sems, (blk + 4 - 8 * way, y))

    def onward(i, source, spot, own):
        target = slot(i, spot, first, second, core)
        arrived = recv.at[i, spot, first, second]
        if own or not late[i]:
            yield remote(source, target, second_send.at[i, spot], arrived, second_device)
        if whole_slice:
            yield remote(source, target, first_send.at[i, spot, 0], arrived, first_device)
        yield remote(
            source, target, core_send.at[i, spot, 0, 0], core_recv.at[i, spot, first, second], to_core
        )

    def after_second(i, spot):
        here = slot(i, spot, first, 1 - second, core)
        if whole_slice:
            yield remote(
                here, here, first_send.at[i, spot, 1], recv.at[i, spot, first, 1 - second], first_device
            )
        yield remote(
            here, here, core_send.at[i, spot, 0, 1], core_recv.at[i, spot, first, 1 - second], to_core
        )

    def after_first(i, spot, turn):
        by_second = second if turn == 0 else 1 - second
        here = slot(i, spot, 1 - first, by_second, core)
        return remote(
            here, here, core_send.at[i, spot, 1, turn], core_recv.at[i, spot, 1 - first, by_second], to_core
        )

    def line_steps():
        for far in range(1, planes):
            yield z - far, z >= far, 0, z < planes - 1
            yield z + far, z < planes - far, 1, z > 0

    ends = [(0, z < planes - 1), (1, z > 0)]
    own_copies = []
    for i in range(count):
        copy = pltpu.make_async_copy(
            shards[i], slot(i, z, first, second, core), own_sem.at[1 + i]
        )
        copy.start()
        own_copies.append(copy)

        for way, further in ends:

            @pl.when(further)
            def _():
                along(i, shards[i], z, 0, way).start()

        for copy in onward(i, shards[i], z, True):
            copy.start()
    rides = rides_of(planes, rides)

    def issue(number):
        for ride in rides:
            ride.issue_more(number)

    issue(6)
    for i in range(count):
        arrive(i, z, first, 1 - second)
        for way, further in ends * late[i]:

            @pl.when(further)
            def _():
                along(i, slot(i, z, first, 1 - second, core), z, 1, way).start()

        for copy in after_second(i, z):
            copy.start()
    issue(4)
    for spot, there, way, further in line_steps():

        @pl.when(there)
        def _():
            for i in range(count):
                here = slot(i, spot, first, second, core)
                arrive(i, spot, first, second)

                @pl.when(further)
                def _():
                    along(i, here, spot, 0, way).start()

                for copy in onward(i, here, spot, False):
                    copy.start()
            for i in range(count):
                arrive(i, spot, first, 1 - second)
                if late[i]:

                    @pl.when(further)
                    def _():
                        along(i, slot(i, spot, first, 1 - second, core), spot, 1, way).start()

                for copy in after_second(i, spot):
                    copy.start()

        issue(4)

    issue(8 * planes)
    spots = [lax.rem(z + at, planes) for at in range(planes)]
    if whole_slice:
        for spot in spots:
            for turn in range(2):
                for i in range(count):
                    arrive(i, spot, 1 - first, second if turn == 0 else 1 - second)
                    after_first(i, spot, turn).start()
    for copy in own_copies:
        copy.wait()
    for i in range(count):
        for spot in range(planes):
            for by_first in range(firsts):
                for by_second in range(2):
                    there = slot(i, spot, by_first, by_second, 1 - core)
                    arrived = core_recv.at[i, spot, by_first, by_second]
                    remote(there, there, own_sem.at[0], arrived, to_core).wait_recv()
    for ride in rides:
        ride.finish()
    for i in range(count):
        for turn in range(1 + late[i]):
            for way, further in ends:

                @pl.when(further)
                def _():
                    along(i, shards[i], z, turn, way).wait_send()

            for spot, there, way, further in line_steps():

                @pl.when(there & further)
                def _():
                    along(i, shards[i], spot, turn, way).wait_send()

        for at, spot in enumerate(spots):
            for copy in onward(i, shards[i], spot, at == 0):
                copy.wait_send()
            for copy in after_second(i, spot):
                copy.wait_send()
            for turn in range(2 * (firsts - 1)):
                after_first(i, spot, turn).wait_send()


def gather_now(shards, planes, whole_slice, collective_id, exchanges=(), late_rows=None):
    parts = []
    for array, shard in enumerate(shards):
        rows = shard.shape[0]
        early = rows - (late_rows[array] if late_rows else 0)
        parts += [(array, 0, early, False)] * (early > 0)
        parts += [(array, early, rows - early, True)] * (early < rows)
    count = len(parts)
    firsts = 2 if whole_slice else 1
    specs = exchange_specs(exchanges)
    dma = pltpu.SemaphoreType.DMA
    grid = (planes, 2, 2, 2) if whole_slice else (planes, 2, 2)
    results = communicate(
        functools.partial(gather_kernel, planes, parts, whole_slice, specs),
        list(shards),
        exchanges,
        [jax.ShapeDtypeStruct((*grid, *shard.shape), shard.dtype) for shard in shards],
        [
            dma((count + 1,)),
            dma((2, count, planes, 2)),
            dma((count, planes)),
            dma((count, planes, 2)),
            dma((count, planes, 2, 2)),
            dma((count, planes, firsts, 2)),
            dma((count, planes, firsts, 2)),
        ],
        planes,
        collective_id,
        200,
        "gather_now",
    )
    places = 4 * planes * firsts
    wholes = [
        whole.reshape(places * shard.shape[0], shard.shape[1])
        for whole, shard in zip(results, shards)
    ]
    return wholes + list(results[len(shards) :])


def scatter_kernel(planes, steps, rows, whole_slice, specs, *refs):
    (partial_ref,), (sum_ref,), scratch, rides = split_refs(refs, 1, 1, specs)
    own, from_core, from_first, from_second, from_below, from_above = scratch[:6]
    load_sem, core_sems, first_sems, second_sems, up_sems, down_sems = scratch[6:]
    blk, z, x, core, y = position()
    firsts = 2 if whole_slice else 1
    to_core = (blk + 1 - 2 * core, y)
    if whole_slice:
        first = y * (1 - core) + x * core
        second = x * (1 - core) + y * core
        core_second = second
        first_device = (blk + core * (2 - 4 * x), y + (1 - core) * (1 - 2 * y))
        second_device = (blk + (1 - core) * (2 - 4 * x), y + core * (1 - 2 * y))
    else:
        first, second = 0, x
        first_device, second_device = None, (blk + 2 - 4 * x, y)
    line = [(blk + 4 * (lax.rem(z + at, planes) - z), y) for at in range(1, planes)]
    nearby = [to_core, second_device] + [first_device] * whole_slice + line
    greet(greeted(specs, nearby))

    def piece(step, by_first, by_second, plane):
        some = pl.ds(pl.multiple_of(step * rows, rows), rows)
        if whole_slice:
            by_x = (1 - plane) * by_second + plane * by_first
            by_y = (1 - plane) * by_first + plane * by_second
            return partial_ref.at[:, by_x, plane, by_y, some]
        return partial_ref.at[:, by_second, plane, some]

    def core_copy(step, by_first, by_second, plane):
        return remote(
            piece(step, by_first, by_second, plane),
            from_core.at[step, by_first, by_second],
            core_sems.at[0, step, by_first, by_second],
            core_sems.at[1, step, by_first, by_second],
            to_core,
        )

    def load(step, by_first, by_second):
        return pltpu.make_async_copy(
            piece(step, by_first, by_second, core),
            own.at[step, by_first, by_second],
            load_sem.at[step, by_first, by_second],
        )

    def first_copy(step):
        return remote(
            own.at[step, 1 - first],
            from_first.at[step],
            first_sems.at[0, step],
            first_sems.at[1, step],
            first_device,
        )

    def second_copy(step):
        return remote(
            own.at[step, first, 1 - second],
            from_second.at[step],
            second_sems.at[0, step],
            second_sems.at[1, step],
            second_device,
        )

    def up_copy(step, target):
        return remote(
            own.at[step, first, second, target],
            from_below.at[step, target],
            up_sems.at[0, step, target],
            up_sems.at[1, step, target],
            (blk + 4, y),
        )

    def down_copy(step, target):
        return remote(
            own.at[step, first, second, target],
            from_above.at[step, target],
            down_sems.at[0, step, target],
            down_sems.at[1, step, target],
            (blk - 4, y),
        )

    def halves():
        if not whole_slice:
            return [(0, 1 - second), (0, second)]
        return [(1 - first, 0), (1 - first, 1), (first, 0), (first, 1)]

    def core_halves():
        if not whole_slice:
            return [(0, 1 - second), (0, second)]
        return [(1 - core_second, 0), (1 - core_second, 1), (core_second, 0), (core_second, 1)]

    def start_loads(step):
        for mine, theirs in zip(halves(), core_halves()):
            core_copy(step, *theirs, 1 - core).start()
            load(step, *mine).start()

    def add_core(step):
        for turn, mine in enumerate(halves()):
            load(step, *mine).wait()
            core_copy(step, *mine, core).wait_recv()
            own[step, *mine] += from_core[step, *mine]
            if whole_slice and turn == 1:
                first_copy(step).start()
            if not whole_slice and turn == 0:
                second_copy(step).start()

    def add_first(step):
        first_copy(step).wait_recv()
        own[step, first, 1 - second] += from_first[step, 1 - second]
        second_copy(step).start()
        own[step, first, second] += from_first[step, second]

    def add_second(step):
        second_copy(step).wait_recv()
        own[step, first, second] += from_second[step]

    def pass_up(step):
        for target in range(planes):

            @pl.when((z > 0) & (z <= target))
            def _():
                up_copy(step, target).wait_recv()

            @pl.when((z > 0) & (z < target))
            def _():
                own[step, first, second, target] += from_below[step, target]

            @pl.when(z < target)
            def _():
                up_copy(step, target).start()

    def pass_down(step):
        for target in range(planes):

            @pl.when((z < planes - 1) & (z >= target))
            def _():
                down_copy(step, target).wait_recv()

            @pl.when((z < planes - 1) & (z > target))
            def _():
                own[step, first, second, target] += from_above[step, target]

            @pl.when(z > target)
            def _():
                down_copy(step, target).start()

    def add_line(step):
        some = pl.ds(pl.multiple_of(step * rows, rows), rows)
        sum_ref[some, :] = own[step, first, second, z]

        @pl.when(z > 0)
        def _():
            sum_ref[some, :] += from_below[step, z]

        @pl.when(z < planes - 1)
        def _():
            sum_ref[some, :] += from_above[step, z]

    start_loads(0)
    start_loads(1)
    rides = rides_of(planes, rides)
    early = firsts + 1
    hurry = [-(-ride.count // steps) for ride in rides]

    @pl.loop(0, steps + early + planes)
    def _(turn):
        def stage(step, work):
            @pl.when((step >= 0) & (step < steps))
            def _():
                work(step)

        @pl.when(turn < steps - 2)
        def _():
            start_loads(turn + 2)

        stage(turn, add_core)
        for ride, number in zip(rides, hurry):
            for at in range(number):
                ride.issue(turn * number + at)
        if whole_slice:
            stage(turn - 1, add_first)
        stage(turn - early + 1, add_second)
        stage(turn - early - z, pass_up)
        stage(turn - early - (planes - 1 - z), pass_down)
        stage(turn - early - planes + 1, add_line)

    @pl.loop(0, steps)
    def _(step):
        for theirs in core_halves():
            core_copy(step, *theirs, 1 - core).wait_send()
        if whole_slice:
            first_copy(step).wait_send()
        second_copy(step).wait_send()
        for target in range(planes):

            @pl.when(z < target)
            def _():
                up_copy(step, target).wait_send()

            @pl.when(z > target)
            def _():
                down_copy(step, target).wait_send()

    for ride in rides:
        ride.finish()


def scatter_now(partial, planes, whole_slice, collective_id, exchanges=()):
    firsts = 2 if whole_slice else 1
    shard_rows = partial.shape[0] // (4 * planes * firsts)
    width = partial.shape[1]
    rows = 16
    steps = shard_rows // rows
    dtype = partial.dtype
    specs = exchange_specs(exchanges)
    dma = pltpu.SemaphoreType.DMA
    grid = (planes, 2, 2, 2) if whole_slice else (planes, 2, 2)
    return communicate(
        functools.partial(scatter_kernel, planes, steps, rows, whole_slice, specs),
        [partial.reshape(*grid, shard_rows, width)],
        exchanges,
        [jax.ShapeDtypeStruct((shard_rows, width), dtype)],
        [
            pltpu.VMEM((steps, firsts, 2, planes, rows, width), dtype),
            pltpu.VMEM((steps, firsts, 2, planes, rows, width), dtype),
            pltpu.VMEM((steps if whole_slice else 1, 2, planes, rows, width), dtype),
            pltpu.VMEM((steps, planes, rows, width), dtype),
            pltpu.VMEM((steps, planes, rows, width), dtype),
            pltpu.VMEM((steps, planes, rows, width), dtype),
            dma((steps, firsts, 2)),
            dma((2, steps, firsts, 2)),
            dma((2, steps)),
            dma((2, steps)),
            dma((2, steps, planes)),
            dma((2, steps, planes)),
        ],
        planes,
        collective_id,
        200,
        "scatter_now",
        out_spec=pltpu.VMEM,
        vmem_limit_bytes=48 * 2**20,
    )


def ffn_pack_kernel(gateup_ref, down_ref, packet_ref):
    for at in range(packet_ref.shape[0]):
        columns = slice(at * HEAD, (at + 1) * HEAD)
        packet_ref[at, :, :HEAD] = gateup_ref[0, :, columns].astype(jnp.bfloat16)
        packet_ref[at, :, HEAD : 2 * HEAD] = gateup_ref[1, :, columns].astype(jnp.bfloat16)
        packet_ref[at, :, 2 * HEAD :] = down_ref[:, columns].astype(jnp.bfloat16)


def ffn_packets(gateup, down):
    row_count = gateup.shape[1]
    blocks, wide = FF // HEAD, 5
    return pl.pallas_call(
        ffn_pack_kernel,
        grid=(blocks // wide,),
        in_specs=[
            pl.BlockSpec((2, row_count, wide * HEAD), lambda j: (0, 0, j)),
            pl.BlockSpec((row_count, wide * HEAD), lambda j: (0, j)),
        ],
        out_specs=pl.BlockSpec((wide, row_count, 3 * HEAD), lambda j: (j, 0, 0)),
        out_shape=jax.ShapeDtypeStruct((blocks, row_count, 3 * HEAD), jnp.bfloat16),
        cost_estimate=pl.CostEstimate(flops=0, bytes_accessed=12 * 2**20, transcendentals=0),
        compiler_params=pltpu.CompilerParams(vmem_limit_bytes=32 * 2**20),
        name="ffn_packets",
    )(gateup, down)


def attn_pack_kernel(qkv_ref, out_ref, packet_ref):
    j = pl.program_id(0)

    @pl.when(j < (H + 2) // 2)
    def _():
        for at in range(2):
            packet_ref[at] = qkv_ref[:, at * HEAD : (at + 1) * HEAD].astype(jnp.bfloat16)

    @pl.when(j >= (H + 2) // 2)
    def _():
        for at in range(2):
            packet_ref[at] = out_ref[:, at * HEAD : (at + 1) * HEAD].astype(jnp.bfloat16)


def attn_packets(qkv, out):
    row_count = qkv.shape[0]
    qkv_last, out_last = (H + 2) // 2 - 1, H // 2 - 1
    return pl.pallas_call(
        attn_pack_kernel,
        grid=(H + 1,),
        in_specs=[
            pl.BlockSpec((row_count, 2 * HEAD), lambda j: (0, jnp.minimum(j, qkv_last))),
            pl.BlockSpec((row_count, 2 * HEAD), lambda j: (0, jnp.clip(j - qkv_last - 1, 0, out_last))),
        ],
        out_specs=pl.BlockSpec((2, row_count, HEAD), lambda j: (j, 0, 0)),
        out_shape=jax.ShapeDtypeStruct((2 * H + 2, row_count, HEAD), jnp.bfloat16),
        cost_estimate=pl.CostEstimate(flops=0, bytes_accessed=4 * 2**20, transcendentals=0),
        name="attn_packets",
    )(qkv, out)


def turn_kernel(grads_ref, others_ref, mom_ref, *refs):
    *results, current_ref = refs
    if len(results) == 1:
        low_ref, turned_ref = results[0].at[:, :HEAD], results[0].at[:, HEAD:]
    else:
        low_ref, turned_ref = results
    grads = grads_ref[...] + others_ref[...].astype(jnp.float32)
    low_ref[...] = grads.astype(jnp.bfloat16)
    moment = momentum_decay * mom_ref[...].astype(jnp.float32) + grads
    moment = moment.astype(jnp.bfloat16).astype(jnp.float32)
    norm_size = jnp.sqrt(jnp.sum(moment * moment, keepdims=True))
    current_ref[...] = (moment / (norm_size + eps_pieces)).T.astype(jnp.bfloat16)

    @pl.loop(0, NS_STEPS)
    def _(sweep_index):
        current = current_ref[...]
        gram_matrix = lax.dot_general(
            current, current, (((1,), (1,)), ((), ())), preferred_element_type=jnp.float32
        ).astype(jnp.bfloat16)
        square = jnp.dot(gram_matrix, gram_matrix, preferred_element_type=jnp.float32)
        mixing = (ns_second * gram_matrix.astype(jnp.float32) + ns_third * square).astype(
            jnp.bfloat16
        )
        turned = jnp.dot(mixing, current, preferred_element_type=jnp.float32)
        current_ref[...] = (ns_first * current.astype(jnp.float32) + turned).astype(jnp.bfloat16)

    turned_ref[...] = current_ref[...].astype(jnp.float32).T.astype(jnp.bfloat16)


def orthogonalize(grads, others, moms, results):
    depth, columns = grads.shape
    block = pl.BlockSpec((depth, HEAD), lambda j: (0, j))
    pieces = columns // HEAD
    return pl.pallas_call(
        turn_kernel,
        grid=(pieces,),
        in_specs=[block] * 3,
        out_specs=[pl.BlockSpec((depth, 2 // results * HEAD), lambda j: (0, j))] * results,
        out_shape=[jax.ShapeDtypeStruct((depth, 2 // results * columns), jnp.bfloat16)] * results,
        scratch_shapes=[pltpu.VMEM((HEAD, depth), jnp.bfloat16)],
        cost_estimate=pl.CostEstimate(
            flops=pieces * 20 * depth * HEAD * HEAD, bytes_accessed=12 * depth * columns, transcendentals=0
        ),
        compiler_params=pltpu.CompilerParams(vmem_limit_bytes=48 * 2**20),
        name="orthogonalize",
    )(grads, others, moms)


def update(rate, weight, mom, grad, turn):
    moment = momentum_decay * mom + grad.astype(jnp.float32)
    new = (1.0 - weight_shrink) * weight - rate * turn.astype(jnp.float32)
    return new, moment, new.astype(jnp.bfloat16)


def ffn_update_kernel(
    grad_ref, turn_ref, w_gateup_ref, mom_gateup_ref, w_down_ref, mom_down_ref, *results
):
    for at in range(grad_ref.shape[0]):
        columns = slice(at * HEAD, (at + 1) * HEAD)
        for part in range(3):
            spot = (part, slice(None), columns) if part < 2 else (slice(None), columns)
            weight_ref, mom_ref = (
                (w_gateup_ref, mom_gateup_ref) if part < 2 else (w_down_ref, mom_down_ref)
            )
            packed = slice(part * HEAD, (part + 1) * HEAD)
            values = update(
                matrix_rate,
                weight_ref[spot],
                mom_ref[spot],
                grad_ref[at, :, packed],
                turn_ref[at, :, packed],
            )
            for ref, value in zip(results[:3] if part < 2 else results[3:], values):
                ref[spot] = value


def ffn_update(grads, turns, w_gateup, mom_gateup, w_down, mom_down):
    row_count = w_gateup.shape[1]
    wide = 3
    packet = pl.BlockSpec((wide, row_count, 3 * HEAD), lambda j: (j, 0, 0))
    gateup = pl.BlockSpec((2, row_count, wide * HEAD), lambda j: (0, 0, j))
    down = pl.BlockSpec((row_count, wide * HEAD), lambda j: (0, j))
    dtypes = (jnp.float32, jnp.float32, jnp.bfloat16)
    return pl.pallas_call(
        ffn_update_kernel,
        grid=(FF // HEAD // wide,),
        in_specs=[packet, packet, gateup, gateup, down, down],
        out_specs=[gateup] * 3 + [down] * 3,
        out_shape=[jax.ShapeDtypeStruct(w_gateup.shape, dtype) for dtype in dtypes]
        + [jax.ShapeDtypeStruct(w_down.shape, dtype) for dtype in dtypes],
        cost_estimate=pl.CostEstimate(flops=0, bytes_accessed=50 * 2**20, transcendentals=0),
        compiler_params=pltpu.CompilerParams(vmem_limit_bytes=48 * 2**20),
        name="ffn_update",
    )(grads, turns, w_gateup, mom_gateup, w_down, mom_down)


def attn_update_kernel(rate, packet_ref, w_ref, mom_ref, *results):
    for at in range(2):
        columns = slice(at * HEAD, (at + 1) * HEAD)
        values = update(
            rate,
            w_ref[:, columns],
            mom_ref[:, columns],
            packet_ref[at, :, :HEAD],
            packet_ref[at, :, HEAD:],
        )
        for ref, value in zip(results, values):
            ref[:, columns] = value


def attn_update(rate, offset, packets, weight, mom):
    row_count = packets.shape[1]
    packet = pl.BlockSpec((2, row_count, 2 * HEAD), lambda j: (j + offset // 2, 0, 0))
    block = pl.BlockSpec((row_count, 2 * HEAD), lambda j: (0, j))
    return pl.pallas_call(
        functools.partial(attn_update_kernel, rate),
        grid=(weight.shape[1] // HEAD // 2,),
        in_specs=[packet, block, block],
        out_specs=[block] * 3,
        out_shape=[
            jax.ShapeDtypeStruct(weight.shape, dtype)
            for dtype in (jnp.float32, jnp.float32, jnp.bfloat16)
        ],
        cost_estimate=pl.CostEstimate(flops=0, bytes_accessed=6 * 2**20, transcendentals=0),
        name="attn_update",
    )(packets, weight, mom)


def two_heads(ref):
    return jnp.concatenate([ref[:, :HEAD], ref[:, HEAD:]], axis=0)


def visible(tokens, first_token, shape, query_axis):
    query = lax.rem(lax.broadcasted_iota(jnp.int32, shape, query_axis), tokens)
    key = lax.broadcasted_iota(jnp.int32, shape, 1 - query_axis)
    distance = query + WINDOW - key
    return (distance >= 0) & (distance < WINDOW) & (first_token - WINDOW + key >= 0)


def attend_kernel(first_ref, queries_ref, kv_ref, mixed_ref, log_total_ref):
    tokens = queries_ref.shape[0]
    raw = lax.dot_general(
        two_heads(queries_ref),
        kv_ref[:, :HEAD],
        (((1,), (1,)), ((), ())),
        preferred_element_type=jnp.float32,
    )
    allowed = visible(tokens, first_ref[0], raw.shape, 0)
    scores = jnp.where(allowed, raw * HEAD ** (-0.5), masked_score)
    top_score = jnp.max(scores, axis=-1, keepdims=True)
    expo = jnp.exp(scores - top_score)
    total = jnp.sum(expo, axis=-1, keepdims=True)
    probs = (expo / total).astype(jnp.bfloat16)
    mixed = jnp.dot(probs, kv_ref[:, HEAD:], preferred_element_type=jnp.float32)
    mixed_ref[:, :HEAD] = mixed[:tokens].astype(jnp.bfloat16)
    mixed_ref[:, HEAD:] = mixed[tokens:].astype(jnp.bfloat16)
    log_total_ref[0] = jnp.broadcast_to(top_score + jnp.log(total), log_total_ref.shape[1:])


def attend(first_token, qkv, kv_window):
    tokens = qkv.shape[0]
    span = kv_window.shape[0]
    pairs = H // 2
    return pl.pallas_call(
        attend_kernel,
        grid=(pairs,),
        in_specs=[
            pl.BlockSpec(memory_space=pltpu.SMEM),
            pl.BlockSpec((tokens, 2 * HEAD), lambda j: (0, j)),
            pl.BlockSpec((span, 2 * HEAD), lambda j: (0, 0)),
        ],
        out_specs=[
            pl.BlockSpec((tokens, 2 * HEAD), lambda j: (0, j)),
            pl.BlockSpec((1, 2 * tokens, 128), lambda j: (j, 0, 0)),
        ],
        out_shape=[
            jax.ShapeDtypeStruct((tokens, H * HEAD), jnp.bfloat16),
            jax.ShapeDtypeStruct((pairs, 2 * tokens, 128), jnp.float32),
        ],
        cost_estimate=pl.CostEstimate(
            flops=4 * H * tokens * span * HEAD,
            bytes_accessed=4 * 2**20,
            transcendentals=H * tokens * span,
        ),
        compiler_params=pltpu.CompilerParams(vmem_limit_bytes=48 * 2**20),
        name="attend",
    )(first_token, qkv, kv_window)


def attend_back_kernel(
    first_ref, queries_ref, grads_ref, log_total_ref, kv_ref, grad_query_ref, grad_kv_ref, sums_ref
):
    tokens = queries_ref.shape[0]
    score_scale = HEAD ** (-0.5)
    keys, values = kv_ref[:, :HEAD], kv_ref[:, HEAD:]
    queries, grads = two_heads(queries_ref), two_heads(grads_ref)

    def against(left, right):
        return lax.dot_general(
            left, right, (((1,), (1,)), ((), ())), preferred_element_type=jnp.float32
        )

    raw = against(keys, queries)
    allowed = visible(tokens, first_ref[0], raw.shape, 1)
    scores = jnp.where(allowed, raw * score_scale, masked_score)
    log_total = log_total_ref[0].T[:1]
    probs = jnp.exp(scores - log_total)
    grad_probs = against(values, grads)
    row_delta = jnp.sum(probs * grad_probs, axis=0, keepdims=True)
    grad_raw = (probs * (grad_probs - row_delta) * score_scale).astype(jnp.bfloat16)
    grad_query = lax.dot_general(
        grad_raw, keys, (((0,), (0,)), ((), ())), preferred_element_type=jnp.float32
    )
    grad_query_ref[:, :HEAD] = grad_query[:tokens].astype(jnp.bfloat16)
    grad_query_ref[:, HEAD:] = grad_query[tokens:].astype(jnp.bfloat16)

    @pl.when(pl.program_id(0) == 0)
    def _():
        sums_ref[...] = jnp.zeros_like(sums_ref)

    sums_ref[:, :HEAD] += jnp.dot(grad_raw, queries, preferred_element_type=jnp.float32)
    sums_ref[:, HEAD:] += jnp.dot(
        probs.astype(jnp.bfloat16), grads, preferred_element_type=jnp.float32
    )

    @pl.when(pl.program_id(0) == pl.num_programs(0) - 1)
    def _():
        grad_kv_ref[...] = sums_ref[...].astype(jnp.bfloat16)


def attend_back(first_token, qkv, grads, log_total, kv_window):
    tokens = qkv.shape[0]
    span = kv_window.shape[0]
    heads = pl.BlockSpec((tokens, 2 * HEAD), lambda j: (0, j))
    window = pl.BlockSpec((span, 2 * HEAD), lambda j: (0, 0))
    return pl.pallas_call(
        attend_back_kernel,
        grid=(H // 2,),
        in_specs=[
            pl.BlockSpec(memory_space=pltpu.SMEM),
            heads,
            heads,
            pl.BlockSpec((1, 2 * tokens, 128), lambda j: (j, 0, 0)),
            window,
        ],
        out_specs=[heads, window],
        out_shape=[
            jax.ShapeDtypeStruct((tokens, H * HEAD), jnp.bfloat16),
            jax.ShapeDtypeStruct((span, 2 * HEAD), jnp.bfloat16),
        ],
        scratch_shapes=[pltpu.VMEM((span, 2 * HEAD), jnp.float32)],
        cost_estimate=pl.CostEstimate(
            flops=10 * H * tokens * span * HEAD,
            bytes_accessed=8 * 2**20,
            transcendentals=H * tokens * span,
        ),
        compiler_params=pltpu.CompilerParams(vmem_limit_bytes=48 * 2**20),
        name="attend_back",
    )(first_token, qkv, grads, log_total, kv_window)


def rms_scale(stream, gain_row):
    mean_square = jnp.mean(stream * stream, axis=-1, keepdims=True)
    return stream * lax.rsqrt(mean_square + eps_norm) * gain_row


def gelu_product(gate_part, up_part):
    return jax.nn.gelu(gate_part, approximate=True) * up_part


def on_device(
    tokens_in,
    cotangent,
    w_qkv,
    w_out,
    w_gateup,
    w_down,
    gains,
    mom_qkv,
    mom_out,
    mom_gateup,
    mom_down,
    mom_gains,
):
    everyone = ("blk", "pair")
    bf16 = jnp.bfloat16
    f32 = jnp.float32
    blk_count = lax.axis_size("blk")
    pair_count = lax.axis_size("pair")
    device_count = blk_count * pair_count
    block_at = lax.axis_index("blk")
    half_at = lax.axis_index("pair")
    me = block_at * pair_count + half_at
    local_rows, width = tokens_in.shape
    share_rows = w_qkv.shape[0]
    span = WINDOW + local_rows
    token_count = local_rows * device_count
    large = token_count * width * 2 > 48 * 2**20
    planes = blk_count // 4
    spread = not large

    def after(value, earlier):
        return lax.optimization_barrier((value, earlier))[0] if large else value

    def exchange(packets, axes=everyone):
        return lax.all_to_all(packets, axes, split_axis=0, concat_axis=0, tiled=True)

    def swap(shard):
        return lax.ppermute(shard, "pair", [(0, 1), (1, 0)])

    def hold(value, *earlier):
        return value if large else lax.optimization_barrier((value, earlier))[0]

    def ride(packets, among="all", **options):
        sources = {"all": device_count, "plane": blk_count, "pair": pair_count}[among]
        return Exchange(packets, among, **(dict(sources=sources) | options))

    def exchanged(rides):
        results = []
        for packets, among, _, before, _, _ in rides:
            if among == "pair":
                results.append(swap(packets))
                continue
            axes, places = (everyone, device_count) if among == "all" else ("blk", blk_count)
            after_last = places - before - packets.shape[0]
            packets = jnp.pad(packets, ((before, after_last),) + ((0, 0),) * (packets.ndim - 1))
            results.append(exchange(packets, axes))
        return results

    def gather(shards, whole_slice, collective_id, rides=(), **options):
        if large:
            axes = everyone if whole_slice else "blk"
            wholes = [lax.all_gather(shard, axes, axis=0, tiled=True) for shard in shards]
            return wholes + exchanged(rides)
        return gather_now(shards, planes, whole_slice, collective_id, rides, **options)

    def scatter(partial, whole_slice, collective_id, rides=()):
        if large:
            axes = everyone if whole_slice else "blk"
            part = lax.psum_scatter(partial, axes, scatter_dimension=0, tiled=True)
            return [part] + exchanged(rides)
        return scatter_now(partial, planes, whole_slice, collective_id, rides)

    def gather_plane(shard):
        return lax.all_gather(shard, "blk", axis=0, tiled=True)

    stream = tokens_in.astype(f32)
    padded_gains = jnp.pad(gains.astype(bf16), ((0, 14), (0, 128 - share_rows)))
    full_qkv, full_gains, full_out, ffn_weights = gather(
        [w_qkv.astype(bf16), padded_gains, w_out.T.astype(bf16)],
        True,
        1,
        [ride(ffn_packets(w_gateup, w_down.T))],
        late_rows=(0, 0, share_rows),
    )
    ffn_weights = ffn_weights.reshape(width, 3 * HEAD)
    full_gains = full_gains.reshape(device_count, 16, 128)[:, :2, :share_rows].astype(f32)
    gain_attn = full_gains[:, 0].reshape(width)
    gain_mlp = full_gains[:, 1].reshape(width)
    normed_attn_f, norm_back_attn = jax.vjp(rms_scale, stream, gain_attn)
    normed_attn = normed_attn_f.astype(bf16)
    qkv = jnp.dot(normed_attn, full_qkv, preferred_element_type=f32).astype(bf16)
    (kv_all,) = gather([qkv[:, H * HEAD :]], True, 2)
    kv_window = lax.dynamic_slice_in_dim(
        jnp.pad(kv_all, ((WINDOW, 0), (0, 0))), me * local_rows, span, 0
    )
    first_token = (me * local_rows).astype(jnp.int32).reshape(1)
    mixed, log_total = attend(first_token, qkv, kv_window)
    resid = stream + jnp.einsum("tc,dc->td", mixed, full_out, preferred_element_type=f32)

    normed_mlp_f, norm_back_mlp = jax.vjp(rms_scale, resid, gain_mlp)
    normed_mlp = normed_mlp_f.astype(bf16)
    normed_mlp_plane, cotangent_plane, other_weights = gather(
        [normed_mlp, cotangent], False, 3, [ride(ffn_weights, "pair")], late_rows=(0, local_rows // 4)
    )
    pair_weights = [ffn_weights, other_weights]
    gates, ups, downs = (
        [weights[:, part * HEAD : (part + 1) * HEAD] for weights in pair_weights]
        for part in range(3)
    )
    owns_block = me < FF // HEAD
    pair_gateup = jnp.where(owns_block, jnp.concatenate(gates + ups, axis=1), 0)
    pair_down = jnp.where(owns_block, jnp.concatenate(downs, axis=1), 0)
    plane_rows = blk_count * local_rows
    both_parts = jnp.dot(normed_mlp_plane, pair_gateup, preferred_element_type=f32)
    pair_width = pair_count * HEAD
    hidden_f, geglu_back = jax.vjp(
        gelu_product, both_parts[:, :pair_width], both_parts[:, pair_width:]
    )
    hidden = hidden_f.astype(bf16)
    grad_hidden = jnp.dot(cotangent_plane, pair_down, preferred_element_type=f32)
    grad_gate, grad_up = geglu_back(grad_hidden)
    grad_gateup = jnp.concatenate([grad_gate.astype(bf16), grad_up.astype(bf16)], axis=1)
    def ffn_gradient(columns):
        gateup_right = jnp.concatenate(
            [grad_gate[:, columns].astype(bf16), grad_up[:, columns].astype(bf16)], axis=1
        )
        down_right = hidden[:, columns]
        return jnp.concatenate(
            [
                jnp.einsum("td,tf->df", normed_mlp_plane, gateup_right, preferred_element_type=f32),
                jnp.einsum("td,tf->df", cotangent_plane, down_right, preferred_element_type=f32),
            ],
            axis=1,
        )

    def pair_columns(columns):
        return columns.reshape(local_rows, -1, pair_width).transpose(1, 0, 2)

    ffn_theirs = ffn_gradient(slice(HEAD, 2 * HEAD)).astype(bf16)
    grad_normed_part = jnp.einsum("tf,df->td", grad_gateup, pair_gateup, preferred_element_type=f32)
    grad_normed_mlp, ffn_others, ffn_moms, attn_moms, out_rights = scatter(
        grad_normed_part.astype(bf16),
        False,
        4,
        [
            ride(ffn_theirs, "pair"),
            ride(ffn_packets(mom_gateup, mom_down.T)),
            ride(attn_packets(mom_qkv, mom_out.T), spread_targets=spread),
            ride(
                pair_columns(mixed), "plane", first_target=(H + 2) // 2, spread_targets=spread
            ),
        ],
    )
    grad_normed_mlp = grad_normed_mlp.astype(f32)

    ffn_grads = ffn_gradient(slice(0, HEAD))
    ffn_low, ffn_turned = orthogonalize(
        ffn_grads, ffn_others, ffn_moms.reshape(width, 3 * HEAD), 2
    )
    ffn_shape = (device_count, share_rows, 3 * HEAD)

    resid_part, gain_grad_mlp = norm_back_mlp(grad_normed_mlp)
    grad_resid = cotangent.astype(f32) + resid_part
    grad_proj = grad_resid.astype(bf16)
    grad_mixed = jnp.dot(grad_proj, full_out, preferred_element_type=f32).astype(bf16)
    grad_query, grad_kv = attend_back(first_token, qkv, grad_mixed, log_total, kv_window)
    grad_kv_all = lax.dynamic_update_slice_in_dim(
        jnp.zeros((WINDOW + token_count, 2 * HEAD), bf16), grad_kv, me * local_rows, 0
    )[WINDOW:]
    grad_kv, ffn_low = scatter(
        grad_kv_all, True, 5, [ride(ffn_low.reshape(ffn_shape), sources=FF // HEAD)]
    )
    grad_qkv = jnp.concatenate([grad_query, grad_kv], axis=1)
    grad_normed_attn = jnp.einsum("tc,dc->td", grad_qkv, full_qkv, preferred_element_type=f32)
    stream_part, gain_grad_attn = norm_back_attn(grad_normed_attn)
    input_grad = grad_resid + stream_part

    branch_part = jnp.einsum(
        "tf,df->td", after(hidden, grad_normed_mlp), pair_down, preferred_element_type=f32
    )
    branch, ffn_turned, qkv_rights = scatter(
        branch_part.astype(bf16),
        False,
        6,
        [
            ride(ffn_turned.reshape(ffn_shape), sources=FF // HEAD),
            ride(pair_columns(grad_qkv), "plane", spread_targets=spread),
        ],
    )
    block_output = (resid + branch.astype(f32)).astype(bf16)
    normed_attn_plane = gather_plane(after(hold(normed_attn, normed_mlp_plane), (ffn_grads, block_output)))
    grad_proj_plane = gather_plane(after(grad_proj, (ffn_grads, block_output)))

    pair_at = spread_place(planes, block_at) if spread else block_at

    def attn_gradient(half, qkv_rights, out_rights):
        def product(lefts, rights):
            rights = rights.reshape(plane_rows, pair_width)
            rights = lax.dynamic_slice_in_dim(rights, half * HEAD, HEAD, 1)
            return jnp.einsum("td,tf->df", lefts, rights, preferred_element_type=f32)

        return lax.cond(
            pair_at < (H + 2) // pair_count,
            lambda: product(normed_attn_plane, qkv_rights),
            lambda: product(grad_proj_plane, out_rights),
        )

    attn_theirs = attn_gradient(1 - half_at, qkv_rights, out_rights).astype(bf16)
    attn_others = swap(attn_theirs)
    attn_grads = attn_gradient(half_at, *hold((qkv_rights, out_rights), attn_theirs))
    updated_ffn = ffn_update(ffn_low, ffn_turned, w_gateup, mom_gateup, w_down.T, mom_down.T)
    (attn_results,) = orthogonalize(
        attn_grads, hold(attn_others, updated_ffn[0]), attn_moms.reshape(width, HEAD), 1
    )
    gain_grads = jnp.stack([gain_grad_attn, gain_grad_mlp], axis=0)
    gain_grads = gain_grads.reshape(2, device_count, share_rows).transpose(1, 0, 2)
    last_rides = [
        ride(
            attn_results.reshape(device_count, share_rows, 2 * HEAD),
            sources=2 * H + 2,
            spread_sources=spread,
        ),
        ride(jnp.pad(gain_grads, ((0, 0), (0, 6), (0, 128 - share_rows)))),
    ]
    if large:
        attn_results, gain_grads = exchanged(last_rides)
    else:
        attn_results, gain_grads = exchange_now(last_rides, planes, 7)
    gain_share = jnp.sum(gain_grads, axis=0)[:2, :share_rows]

    updated_qkv = attn_update(matrix_rate, 0, attn_results, w_qkv, mom_qkv)
    updated_out = attn_update(output_rate, H + 2, attn_results, w_out.T, mom_out.T)
    moment_gains = momentum_decay * mom_gains + gain_share
    new_gains = gains - gain_rate * moment_gains
    return (
        block_output,
        input_grad,
        *updated_qkv,
        *(result.T for result in updated_out),
        *updated_ffn[:3],
        *(result.T for result in updated_ffn[3:]),
        new_gains,
        moment_gains,
        new_gains.astype(bf16),
    )


def solution(mesh):
    placed = (
        P(("blk", "pair"), None),
        P(("blk", "pair"), None),
        P(("blk", "pair"), None),
        P(None, ("blk", "pair")),
        P(None, ("blk", "pair"), None),
        P(None, ("blk", "pair")),
        P(None, ("blk", "pair")),
        P(("blk", "pair"), None),
        P(None, ("blk", "pair")),
        P(None, ("blk", "pair"), None),
        P(None, ("blk", "pair")),
        P(None, ("blk", "pair")),
    )
    return jax.shard_map(
        on_device,
        mesh=mesh,
        in_specs=placed,
        out_specs=(
            P(("blk", "pair"), None),
            P(("blk", "pair"), None),
            P(("blk", "pair"), None),
            P(("blk", "pair"), None),
            P(("blk", "pair"), None),
            P(None, ("blk", "pair")),
            P(None, ("blk", "pair")),
            P(None, ("blk", "pair")),
            P(None, ("blk", "pair"), None),
            P(None, ("blk", "pair"), None),
            P(None, ("blk", "pair"), None),
            P(None, ("blk", "pair")),
            P(None, ("blk", "pair")),
            P(None, ("blk", "pair")),
            P(None, ("blk", "pair")),
            P(None, ("blk", "pair")),
            P(None, ("blk", "pair")),
        ),
        check_vma=False,
    )
```

profile of v0, /device:TPU:0, one launch (start us, length us, event | category | flops | bytes accessed | tf_op | source)
XLA Modules:
  0.0 1157.8 jit_solution(9372682975638379949)
XLA Ops:
  17.2 165.0 %gather_now.3 = (bf16[4,2,2,2,80,3072]{5,4,3,2,1,0:T(8,128)(2,1)}, bf16[4,2,2,2,16,128]{5,4,3,2,1,0:T(8,128)(2,1)}, bf16[4,2,2,2,80,2560]{5,4,3,2,1,0:T(8,128)(2,1)}, bf16[32,80,768]{2,1,0:T(8,128)(2,1)}) custom-call(bf16[80,3072]{1,0:T(8,128)(2,1)} %convert_element_type.85.refs_0_, bf16[16,128]{1,0:T(8,128)(2,1)} %pad.12.refs_1_, ...), custom_call_target="tpu_custom_call" | custom-call | bytes 209715200 | tf_op jit(solution)/shard_map/gather_now/pallas_call | solution.py:267
  185.6 7.9 convolution_convert_fusion.5.queries_ref
  195.1 35.4 %gather_now.4 = bf16[4,2,2,2,128,512]{5,4,3,2,1,0:T(8,128)(2,1)} custom-call(bf16[128,512]{1,0:T(8,128)(2,1)} %slice.86.refs_0_), custom_call_target="tpu_custom_call" | custom-call | bytes 209715200 | tf_op jit(solution)/shard_map/gather_now/pallas_call | solution.py:267
  232.4 11.4 attend.1
  243.9 10.3 multiply_reduce_fusion
  256.6 134.8 %gather_now.5 = (bf16[4,2,2,128,2560]{4,3,2,1,0:T(8,128)(2,1)}, bf16[4,2,2,128,2560]{4,3,2,1,0:T(8,128)(2,1)}, bf16[2560,768]{1,0:T(8,128)(2,1)}) custom-call(bf16[128,2560]{1,0:T(8,128)(2,1)} %multiply_convert_fusion.2.refs_0_, bf16[128,2560]{1,0:T(8,128)(2,1)} %refs_1_.1, bf16[2560,768]{1,0:T(8,128)(2,1)} %bitcast.79), custom_call_target="tpu_custom_call" | custom-call | bytes 209715200 | tf_op jit(solution)/shard_map/gather_now/pallas_call | solution.py:267
  402.2 6.8 attn_packets.1.refs_3_
  409.0 6.1 fusion.58
  415.1 18.5 %fusion.43 = f32[2048,1024]{0,1:T(8,128)} fusion(bf16[2048,2560]{1,0:T(8,128)(2,1)} %bitcast.94, bf16[2560,256]{1,0:T(8,128)(2,1)} %get-tuple-element.176, bf16[2560,256]{1,0:T(8,128)(2,1)} %get-tuple-element.161, bf16[2560,256]{1,0:T(8,128)(2,1)} %get-tuple-element.175, bf16[2560,256]{1,0:T(8,128)(2,1)} %get-tuple-element.162, pred[]{:T(512)S(6)} %lt.24), kind=kOutput, calls=%fused_computation.75 | convolution fusion | flops 10761011200 | bytes 24117248 | tf_op jit(solution)/shard_map/dot_general | solution.py:1212
  433.6 14.4 %fusion.14 = (bf16[2048,512]{0,1:T(8,128)(2,1)S(1)}, bf16[2048,512]{0,1:T(8,128)(2,1)S(1)}, bf16[2048,512]{0,1:T(8,128)(2,1)}) fusion(f32[2048,1024]{0,1:T(8,128)} %fusion.43, bf16[2048,2560]{1,0:T(8,128)(2,1)} %bitcast.101, bf16[2560,256]{1,0:T(8,128)(2,1)} %get-tuple-element.177, bf16[2560,256]{1,0:T(8,128)(2,1)} %get-tuple-element.160, pred[]{:T(512)S(6)} %lt.24), kind=kOutput, calls=%fused_computation.26 | convolution fusion | flops 5402525696 | bytes 27787264 | tf_op jit(solution)/shard_map/dot_general | solution.py:1218
  451.3 7.2 convolution_convert_fusion.3
  458.6 6.4 convolution_convert_fusion.2
  467.2 16.4 %convolution_convert_fusion = bf16[2048,2560]{1,0:T(8,128)(2,1)} fusion(bf16[2048,512]{0,1:T(8,128)(2,1)} %copy-done.32, bf16[2048,512]{0,1:T(8,128)(2,1)S(1)} %get-tuple-element.157, bf16[2560,256]{1,0:T(8,128)(2,1)} %get-tuple-element.176, bf16[2560,256]{1,0:T(8,128)(2,1)} %get-tuple-element.161, bf16[2560,256]{1,0:T(8,128)(2,1)} %get-tuple-element.175, ...), kind=kOutput, calls=%fused_computation.12 | convolution fusion | flops 10774642688 | bytes 19922944 | tf_op jit(solution)/shard_map/tf,df->td/dot_general | solution.py:1238
  483.6 160.5 %scatter_now.3 = (bf16[128,2560]{1,0:T(8,128)(2,1)S(1)}, bf16[2560,768]{1,0:T(8,128)(2,1)}, bf16[32,80,768]{2,1,0:T(8,128)(2,1)}, bf16[32,80,256]{2,1,0:T(8,128)(2,1)S(1)}, bf16[16,128,512]{2,1,0:T(8,128)(2,1)}) custom-call(bf16[4,2,2,128,2560]{4,3,2,1,0:T(8,128)(2,1)} %bitcast.81, bf16[2560,768]{1,0:T(8,128)(2,1)} %pad_maximum_fusion.1.refs_1_, ...), custom_call_target="tpu_custom_call" | custom-call | bytes 209715200 | tf_op jit(solution)/shard_map/scatter_now/pallas_call | solution.py:267
  647.1 6.9 convolution_convert_fusion.4.grads_ref
  654.0 21.1 %attend_back.1 = (bf16[128,2560]{1,0:T(8,128)(2,1)S(1)}, bf16[2176,512]{1,0:T(8,128)(2,1)S(1)}) custom-call(s32[1]{0:T(128)} %bitcast.8.first_ref, bf16[128,3072]{1,0:T(8,128)(2,1)S(1)} %copy-done.17, bf16[128,2560]{1,0:T(8,128)(2,1)S(1)} %convolution_convert_fusion.4.grads_ref, f32[5,256,128]{2,1,0:T(8,128)S(1)} %copy-done.23, bf16[2176,512]{1,0:T(8,128)(2,1)} %copy-done.14), custom_call_target="tpu_custom_call" | custom-call | flops 7130316800 | bytes 8388608 | tf_op jit(solution)/shard_map/attend_back/pallas_call | solution.py:1063
  678.2 6.6 fusion.41
  687.0 5.7 fusion.18
  696.4 37.1 %orthogonalize.2 = (bf16[2560,768]{1,0:T(8,128)(2,1)S(1)}, bf16[2560,768]{1,0:T(8,128)(2,1)}) custom-call(f32[2560,768]{1,0:T(8,128)} %pad_maximum_fusion.grads_ref, bf16[2560,768]{1,0:T(8,128)(2,1)} %get-tuple-element.114.others_ref, bf16[2560,768]{1,0:T(8,128)(2,1)} %bitcast.104), custom_call_target="tpu_custom_call" | custom-call | flops 10066329600 | bytes 23592960 | tf_op jit(solution)/shard_map/orthogonalize/pallas_call | solution.py:861
  735.4 109.7 %scatter_now.4 = (bf16[128,512]{1,0:T(8,128)(2,1)S(1)}, bf16[32,80,768]{2,1,0:T(8,128)(2,1)S(1)}) custom-call(bf16[4,2,2,2,128,512]{5,4,3,2,1,0:T(8,128)(2,1)} %bitcast.77, bf16[32,80,768]{2,1,0:T(8,128)(2,1)} %bitcast.68), custom_call_target="tpu_custom_call" | custom-call | bytes 209715200 | tf_op jit(solution)/shard_map/scatter_now/pallas_call | solution.py:267
  853.2 10.3 convolution_convert_fusion.1
  863.6 148.4 %scatter_now.5 = (bf16[128,2560]{1,0:T(8,128)(2,1)S(1)}, bf16[32,80,768]{2,1,0:T(8,128)(2,1)S(1)}, bf16[16,128,512]{2,1,0:T(8,128)(2,1)}) custom-call(bf16[4,2,2,128,2560]{4,3,2,1,0:T(8,128)(2,1)} %bitcast.82, bf16[32,80,768]{2,1,0:T(8,128)(2,1)} %bitcast.83, bf16[6,128,512]{2,1,0:T(8,128)(2,1)S(1)} %bitcast.69), custom_call_target="tpu_custom_call" | custom-call | bytes 209715200 | tf_op jit(solution)/shard_map/scatter_now/pallas_call | solution.py:267
  1014.7 8.3 conditional.7
  1014.7 8.3 convolution_bitcast_fusion.1
  1028.6 12.3 %fusion.31 = (f32[2560]{0:T(1024)S(1)}, f32[128]{0:T(128)S(1)}, f32[128,2560]{1,0:T(8,128)}) fusion(bf16[128,2560]{1,0:T(8,128)(2,1)} %param.16, f32[128]{0:T(128)S(1)} %copy-done.39, f32[2560]{0:T(1024)S(1)} %copy-done.36, bf16[128,3072]{1,0:T(8,128)(2,1)} %constant_dynamic-update-slice_fusion, bf16[2560,3072]{1,0:T(8,128)(2,1)} %bitcast.74), kind=kOutput, calls=%fused_computation.60 | convolution fusion | flops 2015556992 | bytes 18502656 | tf_op jit(solution)/shard_map/tc,dc->td/dot_general | solution.py:1272
  1043.6 15.9 %ffn_update.1 = (f32[2,80,7680]{2,1,0:T(8,128)}, f32[2,80,7680]{2,1,0:T(8,128)}, bf16[2,80,7680]{2,1,0:T(8,128)(2,1)}, f32[80,7680]{1,0:T(8,128)}, f32[80,7680]{1,0:T(8,128)}, /*index=5*/bf16[80,7680]{1,0:T(8,128)(2,1)}) custom-call(bf16[32,80,768]{2,1,0:T(8,128)(2,1)} %copy-done.7, bf16[32,80,768]{2,1,0:T(8,128)(2,1)} %copy-done.8, ...), custom_call_target="tpu_custom_call" | custom-call | bytes 52428800 | tf_op jit(solution)/shard_map/ffn_update/pallas_call | solution.py:911
  1061.7 12.2 %conditional.8 = (f32[2560,256]{1,0:T(8,128)}) conditional(s32[]{:T(128)} %convert_element_type.101, (bf16[16,128,512]{2,1,0:T(8,128)(2,1)}, s32[]{:T(128)}, bf16[2048,2560]{1,0:T(8,128)(2,1)}) %tuple.37, (bf16[16,128,512]{2,1,0:T(8,128)(2,1)}, s32[]{:T(128)}, bf16[2048,2560]{1,0:T(8,128)(2,1)}) %tuple.38), branch_computations={%region_6.7_spmd, %region_7.8_spmd} | conditional | flops 2684354560 | bytes 19398714 | solution.py:1300
  1061.7 8.8 convolution_bitcast_fusion.3
  1074.0 13.1 %orthogonalize.3 = bf16[2560,512]{1,0:T(8,128)(2,1)S(1)} custom-call(f32[2560,256]{1,0:T(8,128)} %get-tuple-element.147.grads_ref, bf16[2560,256]{1,0:T(8,128)(2,1)} %collective-permute-done.others_ref, bf16[2560,256]{1,0:T(8,128)(2,1)S(1)} %bitcast.72), custom_call_target="tpu_custom_call" | custom-call | flops 3355443200 | bytes 7864320 | tf_op jit(solution)/shard_map/orthogonalize/pallas_call | solution.py:861
  1088.6 51.5 %exchange_now.1 = (bf16[32,80,512]{2,1,0:T(8,128)(2,1)}, f32[32,8,128]{2,1,0:T(8,128)}) custom-call(bf16[32,80,512]{2,1,0:T(8,128)(2,1)} %bitcast.71, f32[32,8,128]{2,1,0:T(8,128)} %pad.14.refs_1_), custom_call_target="tpu_custom_call" | custom-call | bytes 104857600 | tf_op jit(solution)/shard_map/exchange_now/pallas_call | solution.py:267
  1140.1 5.1 attn_update.2
  1145.2 4.6 attn_update.3
  (159 shorter events, 75.6 us)
Async XLA Ops:
  7.2 1007.5 %all-gather.5.cloned.1.call-start = ((), (), s32[]{:S(2)}) async-start(), calls=%async_computation.1 | async-start | bytes 11141120 | tf_op jit(solution)/shard_map/all_gather | solution.py:1172
  16.6 166.7 %copy-start.26 = (bf16[128,2560]{1,0:T(8,128)(2,1)S(1)}, bf16[128,2560]{1,0:T(8,128)(2,1)}, u32[]{:S(2)}) copy-start(bf16[128,2560]{1,0:T(8,128)(2,1)} %param.16) | copy-start | bytes 1966084
  183.3 10.3 copy-start.35
  232.4 11.5 copy-start.14
  232.4 11.5 copy-start.27
  243.9 10.3 copy-start.22
  391.5 623.2 %all-gather.3.cloned.1.call-start = ((), (), s32[]{:S(2)}) async-start(), calls=%async_computation | async-start | bytes 11141120 | tf_op jit(solution)/shard_map/all_gather | solution.py:1172
  449.3 9.2 slice-start
  451.3 7.2 slice-start.1
  451.3 7.2 slice-start.2
  467.1 16.4 %copy-start.10 = (bf16[22,80,256]{2,1,0:T(8,128)(2,1)S(1)}, bf16[22,80,256]{2,1,0:T(8,128)(2,1)}, u32[]{:S(2)}) copy-start(bf16[22,80,256]{2,1,0:T(8,128)(2,1)} %attn_packets.1.refs_3_) | copy-start | bytes 2703364
  467.2 16.4 %copy-start.12 = (bf16[128,5,512]{2,0,1:T(8,128)(2,1)S(1)}, bf16[128,5,512]{2,0,1:T(8,128)(2,1)}, u32[]{:S(2)}) copy-start(bf16[128,5,512]{2,0,1:T(8,128)(2,1)} %copy.40) | copy-start | bytes 1966084
  483.6 161.6 %copy-start.24 = (f32[128,2560]{1,0:T(8,128)S(1)}, f32[128,2560]{1,0:T(8,128)}, u32[]{:S(2)}) copy-start(f32[128,2560]{1,0:T(8,128)} %get-tuple-element.173) | copy-start | bytes 3932164
  483.6 162.1 %copy-start.29 = (bf16[128,2560]{1,0:T(8,128)(2,1)S(1)}, bf16[128,2560]{1,0:T(8,128)(2,1)}, u32[]{:S(2)}) copy-start(bf16[128,2560]{1,0:T(8,128)(2,1)} %refs_1_.1) | copy-start | bytes 1966084
  647.0 6.9 copy-start.17
  647.1 6.9 copy-start.23
  675.8 9.1 slice-start.3
  678.2 6.7 copy-start.33
  678.2 6.7 copy-start.34
  678.2 7.9 slice-start.4
  678.2 8.7 slice-start.5
  853.2 10.3 copy-start.11
  1023.0 5.6 copy-start.36
  1023.0 5.6 copy-start.39
  1025.7 48.3 %collective-permute-start = (bf16[2560,256]{1,0:T(8,128)(2,1)}, bf16[2560,256]{1,0:T(8,128)(2,1)}, u32[]{:S(2)}, u32[]{:S(2)}) collective-permute-start(bf16[2560,256]{1,0:T(8,128)(2,1)} %copy.43), channel_id=1, source_target_pairs={{0,1},{1,0},{2,3},{3,2},{4,5},{5,4},{6,7},{7,6},{8,9},{9,8},{10,11... | collective-permute-start | bytes 3932168 | tf_op jit(solution)/shard_map/ppermute | solution.py:1136
  1043.5 15.9 %copy-start.44 = (f32[128]{0:T(128)S(1)}, f32[128]{0:T(128)}, u32[]{:S(2)}) copy-start(f32[128]{0:T(128)} %copy-done.43) | copy-start | bytes 1540
  1043.5 15.9 %copy-start.19 = (bf16[128,2560]{1,0:T(8,128)(2,1)S(1)}, bf16[128,2560]{1,0:T(8,128)(2,1)}, u32[]{:S(2)}) copy-start(bf16[128,2560]{1,0:T(8,128)(2,1)} %copy-done.18) | copy-start | bytes 1966084
  1043.5 16.0 %copy-start.25 = (f32[128,2560]{1,0:T(8,128)S(1)}, f32[128,2560]{1,0:T(8,128)}, u32[]{:S(2)}) copy-start(f32[128,2560]{1,0:T(8,128)} %get-tuple-element.173) | copy-start | bytes 3932164
  1043.5 16.0 %copy-start.28 = (bf16[128,2560]{1,0:T(8,128)(2,1)S(1)}, bf16[128,2560]{1,0:T(8,128)(2,1)}, u32[]{:S(2)}) copy-start(bf16[128,2560]{1,0:T(8,128)(2,1)} %param.16) | copy-start | bytes 1966084
  1043.5 16.0 %copy-start.30 = (bf16[128,2560]{1,0:T(8,128)(2,1)S(1)}, bf16[128,2560]{1,0:T(8,128)(2,1)}, u32[]{:S(2)}) copy-start(bf16[128,2560]{1,0:T(8,128)(2,1)} %refs_1_.1) | copy-start | bytes 1966084
  1043.5 16.0 %copy-start.31 = (f32[128,2560]{1,0:T(8,128)S(1)}, f32[128,2560]{1,0:T(8,128)}, u32[]{:S(2)}) copy-start(f32[128,2560]{1,0:T(8,128)} %get-tuple-element.174) | copy-start | bytes 3932164
  1061.7 12.3 %copy-start.21 = (bf16[32,80,256]{2,1,0:T(8,128)(2,1)S(1)}, bf16[32,80,256]{2,1,0:T(8,128)(2,1)}, u32[]{:S(2)}) copy-start(bf16[32,80,256]{2,1,0:T(8,128)(2,1)} %copy-done.20) | copy-start | bytes 3932164
  (24 other events, 54.4 us)
Sparse Core Ops, SparseCore 0:
  391.6 84.3 all-gather.4
  647.2 86.3 all-gather.2
where the time goes:
time: 1160 us
  Pallas kernels  923 us (80%)
  matrix products  140 us (12%)
  local copies, waits for them, and re-layouts  57.2 us (5%)
  other arithmetic  19.3 us (2%)
  between operations  15.2 us (1%)
    pallas_call x7, Pallas kernels, communicate(): pl.pallas_call(kernel, out_shape=outputs + received, in_specs=[any_spec]...  805 us
    pallas_call x2, Pallas kernels, orthogonalize(): pl.pallas_call(turn_kernel, grid=(pieces,), in_specs=[block] * 3, out_spe...  50.2 us
    unnamed x107, local copies, waits for them, and re-layouts  27.1 us
  transfers between devices with their start and end apart: 3, of which 0 were waited for; matrix products, arithmetic and copies ran while one was open for 13% of the time, Pallas kernels for 43%

commit v1 on v0

--- a/solution.py
+++ b/solution.py
@@ -524,10 +524,14 @@
     return wholes + list(results[len(shards) :])
 
 
-def scatter_kernel(planes, steps, rows, whole_slice, specs, *refs):
-    (partial_ref,), (sum_ref,), scratch, rides = split_refs(refs, 1, 1, specs)
+def scatter_kernel(planes, steps, rows, whole_slice, product, specs, *refs):
+    operands, (sum_ref,), scratch, rides = split_refs(refs, 1 + product, 1, specs)
     own, from_core, from_first, from_second, from_below, from_above = scratch[:6]
-    load_sem, core_sems, first_sems, second_sems, up_sems, down_sems = scratch[6:]
+    load_sem, core_sems, first_sems, second_sems, up_sems, down_sems = scratch[6:12]
+    if product:
+        lefts, rights, made, factor_sems = scratch[12:]
+    else:
+        (partial_ref,) = operands
     blk, z, x, core, y = position()
     firsts = 2 if whole_slice else 1
     to_core = (blk + 1 - 2 * core, y)
@@ -544,7 +548,26 @@
     nearby = [to_core, second_device] + [first_device] * whole_slice + line
     greet(greeted(specs, nearby))
 
+    def make(step):
+        some = pl.ds(pl.multiple_of(step * rows, rows), rows)
+        left = lefts[:, :, :, some, :].reshape(4 * planes * rows, lefts.shape[-1])
+        wide = 2 * HEAD
+
+        @pl.loop(0, rights.shape[0] // wide)
+        def _(at):
+            columns = pl.ds(pl.multiple_of(at * wide, wide), wide)
+            part = lax.dot_general(
+                left,
+                rights[columns, :],
+                (((1,), (1,)), ((), ())),
+                preferred_element_type=jnp.float32,
+            )
+            part = part.astype(made.dtype).reshape(planes, 2, 2, rows, wide)
+            made[step, :, :, :, :, columns] = part
+
     def piece(step, by_first, by_second, plane):
+        if product:
+            return made.at[step, :, by_second, plane]
         some = pl.ds(pl.multiple_of(step * rows, rows), rows)
         if whole_slice:
             by_x = (1 - plane) * by_second + plane * by_first
@@ -615,15 +638,22 @@
         return [(1 - core_second, 0), (1 - core_second, 1), (core_second, 0), (core_second, 1)]
 
     def start_loads(step):
+        if product:
+            make(step)
         for mine, theirs in zip(halves(), core_halves()):
             core_copy(step, *theirs, 1 - core).start()
-            load(step, *mine).start()
+            if not product:
+                load(step, *mine).start()
 
     def add_core(step):
         for turn, mine in enumerate(halves()):
-            load(step, *mine).wait()
+            if not product:
+                load(step, *mine).wait()
             core_copy(step, *mine, core).wait_recv()
-            own[step, *mine] += from_core[step, *mine]
+            if product:
+                own[step, *mine] = made[step, :, mine[1], core] + from_core[step, *mine]
+            else:
+                own[step, *mine] += from_core[step, *mine]
             if whole_slice and turn == 1:
                 first_copy(step).start()
             if not whole_slice and turn == 0:
@@ -681,9 +711,21 @@
         def _():
             sum_ref[some, :] += from_above[step, z]
 
-    start_loads(0)
-    start_loads(1)
     rides = rides_of(planes, rides)
+    if product:
+        factors = [
+            pltpu.make_async_copy(operand, ref, factor_sems.at[i])
+            for i, (operand, ref) in enumerate(zip(operands, (lefts, rights)))
+        ]
+        for factor in factors:
+            factor.start()
+        for factor in factors:
+            factor.wait()
+
+    @pl.loop(0, 2)
+    def _(step):
+        start_loads(step)
+
     early = firsts + 1
     hurry = [-(-ride.count // steps) for ride in rides]
 
@@ -730,19 +772,20 @@
         ride.finish()
 
 
-def scatter_now(partial, planes, whole_slice, collective_id, exchanges=()):
+def scatter_now(factors, planes, whole_slice, collective_id, exchanges=()):
     firsts = 2 if whole_slice else 1
-    shard_rows = partial.shape[0] // (4 * planes * firsts)
-    width = partial.shape[1]
+    product = len(factors) == 2
+    shard_rows = factors[0].shape[0] // (4 * planes * firsts)
+    width = factors[1].shape[0] if product else factors[0].shape[1]
     rows = 16
     steps = shard_rows // rows
-    dtype = partial.dtype
+    dtype = factors[0].dtype
     specs = exchange_specs(exchanges)
     dma = pltpu.SemaphoreType.DMA
     grid = (planes, 2, 2, 2) if whole_slice else (planes, 2, 2)
     return communicate(
-        functools.partial(scatter_kernel, planes, steps, rows, whole_slice, specs),
-        [partial.reshape(*grid, shard_rows, width)],
+        functools.partial(scatter_kernel, planes, steps, rows, whole_slice, product, specs),
+        [factors[0].reshape(*grid, shard_rows, factors[0].shape[1]), *factors[1:]],
         exchanges,
         [jax.ShapeDtypeStruct((shard_rows, width), dtype)],
         [
@@ -758,13 +801,20 @@
             dma((2, steps)),
             dma((2, steps, planes)),
             dma((2, steps, planes)),
-        ],
+        ]
+        + [
+            pltpu.VMEM((*grid, shard_rows, factors[0].shape[1]), dtype),
+            pltpu.VMEM(factors[-1].shape, dtype),
+            pltpu.VMEM((steps, *grid, rows, width), dtype),
+            dma((2,)),
+        ]
+        * product,
         planes,
         collective_id,
         200,
         "scatter_now",
         out_spec=pltpu.VMEM,
-        vmem_limit_bytes=48 * 2**20,
+        vmem_limit_bytes=56 * 2**20,
     )
 
 
@@ -1161,12 +1211,15 @@
             return wholes + exchanged(rides)
         return gather_now(shards, planes, whole_slice, collective_id, rides, **options)
 
-    def scatter(partial, whole_slice, collective_id, rides=()):
+    def scatter(factors, whole_slice, collective_id, rides=()):
         if large:
             axes = everyone if whole_slice else "blk"
-            part = lax.psum_scatter(partial, axes, scatter_dimension=0, tiled=True)
+            if len(factors) == 2:
+                partial = jnp.einsum("tf,df->td", *factors, preferred_element_type=f32)
+                factors = [partial.astype(bf16)]
+            part = lax.psum_scatter(factors[0], axes, scatter_dimension=0, tiled=True)
             return [part] + exchanged(rides)
-        return scatter_now(partial, planes, whole_slice, collective_id, rides)
+        return scatter_now(factors, planes, whole_slice, collective_id, rides)
 
     def gather_plane(shard):
         return lax.all_gather(shard, "blk", axis=0, tiled=True)
@@ -1235,9 +1288,8 @@
         return columns.reshape(local_rows, -1, pair_width).transpose(1, 0, 2)
 
     ffn_theirs = ffn_gradient(slice(HEAD, 2 * HEAD)).astype(bf16)
-    grad_normed_part = jnp.einsum("tf,df->td", grad_gateup, pair_gateup, preferred_element_type=f32)
     grad_normed_mlp, ffn_others, ffn_moms, attn_moms, out_rights = scatter(
-        grad_normed_part.astype(bf16),
+        [grad_gateup, pair_gateup],
         False,
         4,
         [
@@ -1266,18 +1318,15 @@
         jnp.zeros((WINDOW + token_count, 2 * HEAD), bf16), grad_kv, me * local_rows, 0
     )[WINDOW:]
     grad_kv, ffn_low = scatter(
-        grad_kv_all, True, 5, [ride(ffn_low.reshape(ffn_shape), sources=FF // HEAD)]
+        [grad_kv_all], True, 5, [ride(ffn_low.reshape(ffn_shape), sources=FF // HEAD)]
     )
     grad_qkv = jnp.concatenate([grad_query, grad_kv], axis=1)
     grad_normed_attn = jnp.einsum("tc,dc->td", grad_qkv, full_qkv, preferred_element_type=f32)
     stream_part, gain_grad_attn = norm_back_attn(grad_normed_attn)
     input_grad = grad_resid + stream_part
 
-    branch_part = jnp.einsum(
-        "tf,df->td", after(hidden, grad_normed_mlp), pair_down, preferred_element_type=f32
-    )
     branch, ffn_turned, qkv_rights = scatter(
-        branch_part.astype(bf16),
+        [after(hidden, grad_normed_mlp), pair_down],
         False,
         6,
         [

time: 1160 us -> 1150 us (level)
  matrix products: 140 us -> 110 us
  Pallas kernels: 923 us -> 940 us
  local copies, waits for them, and re-layouts: 57.2 us -> 45.6 us
    dot_general x2 -> x0, matrix products: 26.8 us -> none  [the longest x1 16.4 us: on_device(): jnp.einsum('tf,df->td', grad_gateup, pair_gateup, preferred_element_type=...]
    pallas_call x7, Pallas kernels: 805 us -> 823 us  [communicate(): pl.pallas_call(kernel, out_shape=outputs + received, in_specs=[any_spec]...]
    unnamed x107 -> x91, local copies, waits for them, and re-layouts: 27.1 us -> 19.8 us
  transfers between devices with their start and end apart: 3 -> 3, of which waited for: 0 -> 0; matrix products, arithmetic and copies ran while one was open for 13% -> 10% of each run, Pallas kernels for 43% -> 46%
where the time goes in v1:
time: 1150 us; the launch traced here: 1140 us
  Pallas kernels  940 us (82%)
  matrix products  110 us (10%)
  local copies, waits for them, and re-layouts  45.6 us (4%)
  other arithmetic  25.9 us (2%)
  between operations  15.2 us (1%)
    pallas_call x7, Pallas kernels, communicate(): pl.pallas_call(kernel, out_shape=outputs + received, in_specs=[any_spec]...  823 us
    pallas_call x2, Pallas kernels, orthogonalize(): pl.pallas_call(turn_kernel, grid=(pieces,), in_specs=[block] * 3, out_spe...  50.3 us
  transfers between devices with their start and end apart: 3, of which 0 were waited for; matrix products, arithmetic and copies ran while one was open for 10% of the time, Pallas kernels for 46%

profile of v1, /device:TPU:0, one launch (start us, length us, event | category | flops | bytes accessed | tf_op | source)
XLA Modules:
  0.0 1139.5 jit_solution(7644159888076086679)
XLA Ops:
  17.2 165.0 %gather_now.3 = (bf16[4,2,2,2,80,3072]{5,4,3,2,1,0:T(8,128)(2,1)}, bf16[4,2,2,2,16,128]{5,4,3,2,1,0:T(8,128)(2,1)}, bf16[4,2,2,2,80,2560]{5,4,3,2,1,0:T(8,128)(2,1)}, bf16[32,80,768]{2,1,0:T(8,128)(2,1)}) custom-call(bf16[80,3072]{1,0:T(8,128)(2,1)} %convert_element_type.79.refs_0_, bf16[16,128]{1,0:T(8,128)(2,1)} %pad.12.refs_1_, ...), custom_call_target="tpu_custom_call" | custom-call | bytes 209715200 | tf_op jit(solution)/shard_map/gather_now/pallas_call | solution.py:267
  185.6 7.9 convolution_convert_fusion.3.queries_ref
  195.1 35.4 %gather_now.4 = bf16[4,2,2,2,128,512]{5,4,3,2,1,0:T(8,128)(2,1)} custom-call(bf16[128,512]{1,0:T(8,128)(2,1)} %slice.86.refs_0_), custom_call_target="tpu_custom_call" | custom-call | bytes 209715200 | tf_op jit(solution)/shard_map/gather_now/pallas_call | solution.py:267
  232.4 11.4 %attend.1 = (bf16[128,2560]{1,0:T(8,128)(2,1)S(1)}, f32[5,256,128]{2,1,0:T(8,128)S(1)}) custom-call(s32[1]{0:T(128)} %bitcast.8.first_ref, bf16[128,3072]{1,0:T(8,128)(2,1)S(1)} %copy-done.11, bf16[2176,512]{1,0:T(8,128)(2,1)S(1)} %pad_dynamic-slice_fusion.kv_ref), custom_call_target="tpu_custom_call" | custom-call | flops 2852126720 | bytes 4194304 | tf_op jit(solution)/shard_map/attend/pallas_call | solution.py:1041
  243.9 10.3 multiply_reduce_fusion
  256.6 134.8 %gather_now.5 = (bf16[4,2,2,128,2560]{4,3,2,1,0:T(8,128)(2,1)}, bf16[4,2,2,128,2560]{4,3,2,1,0:T(8,128)(2,1)}, bf16[2560,768]{1,0:T(8,128)(2,1)}) custom-call(bf16[128,2560]{1,0:T(8,128)(2,1)} %multiply_convert_fusion.2.refs_0_, bf16[128,2560]{1,0:T(8,128)(2,1)} %refs_1_.1, bf16[2560,768]{1,0:T(8,128)(2,1)} %bitcast.79), custom_call_target="tpu_custom_call" | custom-call | bytes 209715200 | tf_op jit(solution)/shard_map/gather_now/pallas_call | solution.py:267
  402.3 6.8 attn_packets.1.refs_4_
  409.1 3.8 fusion.43
  416.7 13.2 %fusion.47 = f32[2048,1024]{1,0:T(8,128)} fusion(bf16[2048,2560]{1,0:T(8,128)(2,1)S(1)} %bitcast.98, bf16[2560,1024]{1,0:T(8,128)(2,1)S(1)} %maximum_select_fusion.refs_1_), kind=kOutput, calls=%fused_computation.92 | convolution fusion | flops 10737418240 | bytes 24117248 | tf_op jit(solution)/shard_map/dot_general | solution.py:1265
  429.9 14.7 %fusion.14 = (bf16[2048,512]{1,0:T(8,128)(2,1)S(1)}, bf16[2048,512]{1,0:T(8,128)(2,1)S(1)}, bf16[2048,512]{1,0:T(8,128)(2,1)S(1)}) fusion(f32[2048,1024]{1,0:T(8,128)} %fusion.47, bf16[2048,2560]{1,0:T(8,128)(2,1)} %bitcast.100, bf16[2560,512]{1,0:T(8,128)(2,1)S(1)} %maximum_select_fusion.1.refs_1_), kind=kOutput, calls=%fused_computation.24 | convolution fusion | flops 5395972096 | bytes 27787264 | tf_op jit(solution)/shard_map/dot_general | solution.py:1271
  448.6 7.0 convolution_convert_fusion.1
  455.6 5.9 convolution_convert_fusion
  463.8 170.1 %scatter_now.3 = (bf16[128,2560]{1,0:T(8,128)(2,1)}, bf16[2560,768]{1,0:T(8,128)(2,1)}, bf16[32,80,768]{2,1,0:T(8,128)(2,1)}, bf16[32,80,256]{2,1,0:T(8,128)(2,1)}, bf16[16,128,512]{2,1,0:T(8,128)(2,1)}) custom-call(bf16[4,2,2,128,1024]{4,3,2,1,0:T(8,128)(2,1)} %bitcast.78, bf16[2560,1024]{1,0:T(8,128)(2,1)} %copy-done.18, ...), custom_call_target="tpu_custom_call" | custom-call | bytes 209715200 | tf_op jit(solution)/shard_map/scatter_now/pallas_call | solution.py:267
  638.0 6.9 convolution_convert_fusion.2.grads_ref
  645.0 21.3 %attend_back.1 = (bf16[128,2560]{1,0:T(8,128)(2,1)S(1)}, bf16[2176,512]{1,0:T(8,128)(2,1)S(1)}) custom-call(s32[1]{0:T(128)} %bitcast.8.first_ref, bf16[128,3072]{1,0:T(8,128)(2,1)S(1)} %copy-done.12, bf16[128,2560]{1,0:T(8,128)(2,1)S(1)} %convolution_convert_fusion.2.grads_ref, f32[5,256,128]{2,1,0:T(8,128)S(1)} %copy-done.15, bf16[2176,512]{1,0:T(8,128)(2,1)} %copy-done.9), custom_call_target="tpu_custom_call" | custom-call | flops 7130316800 | bytes 8388608 | tf_op jit(solution)/shard_map/attend_back/pallas_call | solution.py:1113
  669.4 5.7 fusion.35
  675.1 8.5 fusion.15
  683.6 3.8 pad_maximum_fusion.grads_ref
  687.5 37.3 %orthogonalize.2 = (bf16[2560,768]{1,0:T(8,128)(2,1)S(1)}, bf16[2560,768]{1,0:T(8,128)(2,1)}) custom-call(f32[2560,768]{1,0:T(8,128)} %pad_maximum_fusion.grads_ref, bf16[2560,768]{1,0:T(8,128)(2,1)} %get-tuple-element.114.others_ref, bf16[2560,768]{1,0:T(8,128)(2,1)} %bitcast.103), custom_call_target="tpu_custom_call" | custom-call | flops 10066329600 | bytes 23592960 | tf_op jit(solution)/shard_map/orthogonalize/pallas_call | solution.py:911
  726.6 110.6 %scatter_now.4 = (bf16[128,512]{1,0:T(8,128)(2,1)}, bf16[32,80,768]{2,1,0:T(8,128)(2,1)}) custom-call(bf16[4,2,2,2,128,512]{5,4,3,2,1,0:T(8,128)(2,1)} %bitcast.76, bf16[32,80,768]{2,1,0:T(8,128)(2,1)} %bitcast.69), custom_call_target="tpu_custom_call" | custom-call | bytes 209715200 | tf_op jit(solution)/shard_map/scatter_now/pallas_call | solution.py:267
  841.7 155.6 %scatter_now.5 = (bf16[128,2560]{1,0:T(8,128)(2,1)}, bf16[32,80,768]{2,1,0:T(8,128)(2,1)}, bf16[16,128,512]{2,1,0:T(8,128)(2,1)}) custom-call(bf16[4,2,2,128,512]{4,3,2,1,0:T(8,128)(2,1)} %bitcast.89, bf16[2560,512]{1,0:T(8,128)(2,1)} %copy-done.22, bf16[32,80,768]{2,1,0:T(8,128)(2,1)} %bitcast.81, bf16[6,128,512]{2,1,0:T(8,128)(2,1)} %bitcast.85), custom_call_target="tpu_custom_call" | custom-call | bytes 209715200 | tf_op jit(solution)/shard_map/scatter_now/pallas_call | solution.py:267
  997.3 8.3 conditional.7
  997.3 8.3 convolution_bitcast_fusion.1
  1010.4 12.2 %fusion.27 = (f32[2560]{0:T(1024)S(1)}, f32[128]{0:T(128)S(1)}, f32[128,2560]{1,0:T(8,128)}) fusion(bf16[128,2560]{1,0:T(8,128)(2,1)S(1)} %copy-done.21, f32[128]{0:T(128)S(1)} %copy-done.36, f32[2560]{0:T(1024)S(1)} %copy-done.33, bf16[128,3072]{1,0:T(8,128)(2,1)} %copy-done.23, bf16[2560,3072]{1,0:T(8,128)(2,1)} %bitcast.73), kind=kOutput, calls=%fused_computation.55 | convolution fusion | flops 2015556992 | bytes 18502656 | tf_op jit(solution)/shard_map/tc,dc->td/dot_general | solution.py:1324
  1025.3 15.9 %ffn_update.1 = (f32[2,80,7680]{2,1,0:T(8,128)}, f32[2,80,7680]{2,1,0:T(8,128)}, bf16[2,80,7680]{2,1,0:T(8,128)(2,1)}, f32[80,7680]{1,0:T(8,128)}, f32[80,7680]{1,0:T(8,128)}, /*index=5*/bf16[80,7680]{1,0:T(8,128)(2,1)}) custom-call(bf16[32,80,768]{2,1,0:T(8,128)(2,1)} %get-tuple-element.129.grad_ref, bf16[32,80,768]{2,1,0:T(8,128)(2,1)} %get-tuple-element.130.turn_ref, ...), custom_call_target="tpu_custom_call" | custom-call | bytes 52428800 | tf_op jit(solution)/shard_map/ffn_update/pallas_call | solution.py:961
  1043.4 12.3 %conditional.8 = (f32[2560,256]{1,0:T(8,128)}) conditional(s32[]{:T(128)} %convert_element_type.93, (bf16[16,128,512]{2,1,0:T(8,128)(2,1)}, s32[]{:T(128)}, bf16[2048,2560]{1,0:T(8,128)(2,1)}) %tuple.37, (bf16[16,128,512]{2,1,0:T(8,128)(2,1)}, s32[]{:T(128)}, bf16[2048,2560]{1,0:T(8,128)(2,1)}) %tuple.38), branch_computations={%region_6.7_spmd, %region_7.8_spmd} | conditional | flops 2684354560 | bytes 19398714 | solution.py:1349
  1043.4 8.8 convolution_bitcast_fusion.3
  1052.2 3.2 copy.55
  1055.8 13.1 %orthogonalize.3 = bf16[2560,512]{1,0:T(8,128)(2,1)S(1)} custom-call(f32[2560,256]{1,0:T(8,128)} %get-tuple-element.147.grads_ref, bf16[2560,256]{1,0:T(8,128)(2,1)} %collective-permute-done.others_ref, bf16[2560,256]{1,0:T(8,128)(2,1)S(1)} %bitcast.71), custom_call_target="tpu_custom_call" | custom-call | flops 3355443200 | bytes 7864320 | tf_op jit(solution)/shard_map/orthogonalize/pallas_call | solution.py:911
  1070.3 51.5 %exchange_now.1 = (bf16[32,80,512]{2,1,0:T(8,128)(2,1)}, f32[32,8,128]{2,1,0:T(8,128)}) custom-call(bf16[32,80,512]{2,1,0:T(8,128)(2,1)} %bitcast.70, f32[32,8,128]{2,1,0:T(8,128)} %pad.14.refs_1_), custom_call_target="tpu_custom_call" | custom-call | bytes 104857600 | tf_op jit(solution)/shard_map/exchange_now/pallas_call | solution.py:267
  1121.8 5.1 attn_update.2
  1127.0 4.6 attn_update.3
  (143 shorter events, 65.1 us)
Async XLA Ops:
  7.2 4.2 copy-start.37
  7.2 990.1 %all-gather.5.cloned.1.call-start = ((), (), s32[]{:S(2)}) async-start(), calls=%async_computation.1 | async-start | bytes 11141120 | tf_op jit(solution)/shard_map/all_gather | solution.py:1225
  16.6 166.7 %copy-start.19 = (bf16[128,2560]{1,0:T(8,128)(2,1)S(1)}, bf16[128,2560]{1,0:T(8,128)(2,1)}, u32[]{:S(2)}) copy-start(bf16[128,2560]{1,0:T(8,128)(2,1)} %param.16) | copy-start | bytes 1966084
  183.3 10.2 copy-start.32
  232.4 11.5 %copy-start.9 = (bf16[2176,512]{1,0:T(8,128)(2,1)}, bf16[2176,512]{1,0:T(8,128)(2,1)S(1)}, u32[]{:S(2)}) copy-start(bf16[2176,512]{1,0:T(8,128)(2,1)S(1)} %pad_dynamic-slice_fusion.kv_ref) | copy-start | bytes 6684676
  232.4 11.5 %copy-start.20 = (bf16[128,2560]{1,0:T(8,128)(2,1)S(1)}, bf16[128,2560]{1,0:T(8,128)(2,1)}, u32[]{:S(2)}) copy-start(bf16[128,2560]{1,0:T(8,128)(2,1)} %param.16) | copy-start | bytes 1966084
  243.9 10.4 copy-start.14
  391.5 605.8 %all-gather.3.cloned.1.call-start = ((), (), s32[]{:S(2)}) async-start(), calls=%async_computation | async-start | bytes 11141120 | tf_op jit(solution)/shard_map/all_gather | solution.py:1225
  409.1 5.6 slice-start
  409.1 6.9 slice-start.1
  413.4 16.5 %copy-start.22 = (bf16[2560,512]{1,0:T(8,128)(2,1)}, bf16[2560,512]{1,0:T(8,128)(2,1)S(1)}, u32[]{:S(2)}) copy-start(bf16[2560,512]{1,0:T(8,128)(2,1)S(1)} %maximum_select_fusion.1.refs_1_) | copy-start | bytes 7864324
  416.7 13.2 %copy-start.18 = (bf16[2560,1024]{1,0:T(8,128)(2,1)}, bf16[2560,1024]{1,0:T(8,128)(2,1)S(1)}, u32[]{:S(2)}) copy-start(bf16[2560,1024]{1,0:T(8,128)(2,1)S(1)} %maximum_select_fusion.refs_1_) | copy-start | bytes 15728644
  463.7 170.1 %copy-start.16 = (f32[128,2560]{1,0:T(8,128)S(1)}, f32[128,2560]{1,0:T(8,128)}, u32[]{:S(2)}) copy-start(f32[128,2560]{1,0:T(8,128)} %get-tuple-element.173) | copy-start | bytes 3932164
  463.8 171.8 %copy-start.24 = (bf16[128,2560]{1,0:T(8,128)(2,1)S(1)}, bf16[128,2560]{1,0:T(8,128)(2,1)}, u32[]{:S(2)}) copy-start(bf16[128,2560]{1,0:T(8,128)(2,1)} %refs_1_.1) | copy-start | bytes 1966084
  638.0 6.9 copy-start.12
  638.0 6.9 copy-start.15
  669.4 5.8 copy-start.30
  838.2 159.0 %copy-start.23 = (bf16[128,3072]{1,0:T(8,128)(2,1)}, bf16[128,3072]{1,0:T(8,128)(2,1)S(1)}, u32[]{:S(2)}) copy-start(bf16[128,3072]{1,0:T(8,128)(2,1)S(1)} %constant_dynamic-update-slice_fusion) | copy-start | bytes 2359300
  1005.6 4.8 copy-start.21
  1005.6 4.8 copy-start.33
  1005.6 4.8 copy-start.36
  1008.3 47.4 %collective-permute-start = (bf16[2560,256]{1,0:T(8,128)(2,1)}, bf16[2560,256]{1,0:T(8,128)(2,1)}, u32[]{:S(2)}, u32[]{:S(2)}) collective-permute-start(bf16[2560,256]{1,0:T(8,128)(2,1)} %copy.47), channel_id=1, source_target_pairs={{0,1},{1,0},{2,3},{3,2},{4,5},{5,4},{6,7},{7,6},{8,9},{9,8},{10,11... | collective-permute-start | bytes 3932168 | tf_op jit(solution)/shard_map/ppermute | solution.py:1186
  1025.2 15.9 %copy-start.41 = (f32[128]{0:T(128)S(1)}, f32[128]{0:T(128)}, u32[]{:S(2)}) copy-start(f32[128]{0:T(128)} %copy-done.40) | copy-start | bytes 1540
  1025.2 15.9 %copy-start.17 = (f32[128,2560]{1,0:T(8,128)S(1)}, f32[128,2560]{1,0:T(8,128)}, u32[]{:S(2)}) copy-start(f32[128,2560]{1,0:T(8,128)} %get-tuple-element.173) | copy-start | bytes 3932164
  1025.2 16.0 %copy-start.25 = (bf16[128,2560]{1,0:T(8,128)(2,1)S(1)}, bf16[128,2560]{1,0:T(8,128)(2,1)}, u32[]{:S(2)}) copy-start(bf16[128,2560]{1,0:T(8,128)(2,1)} %refs_1_.1) | copy-start | bytes 1966084
  1025.2 16.0 %copy-start.26 = (bf16[128,2560]{1,0:T(8,128)(2,1)S(1)}, bf16[128,2560]{1,0:T(8,128)(2,1)}, u32[]{:S(2)}) copy-start(bf16[128,2560]{1,0:T(8,128)(2,1)} %get-tuple-element.117) | copy-start | bytes 1966084
  1025.3 16.0 %copy-start.27 = (f32[128,2560]{1,0:T(8,128)S(1)}, f32[128,2560]{1,0:T(8,128)}, u32[]{:S(2)}) copy-start(f32[128,2560]{1,0:T(8,128)} %get-tuple-element.174) | copy-start | bytes 3932164
  1025.3 16.0 %copy-start.31 = (bf16[128,2560]{1,0:T(8,128)(2,1)S(1)}, bf16[128,2560]{1,0:T(8,128)(2,1)}, u32[]{:S(2)}) copy-start(bf16[128,2560]{1,0:T(8,128)(2,1)} %get-tuple-element.123) | copy-start | bytes 1966084
  1043.4 12.3 %copy-start.13 = (bf16[32,80,256]{2,1,0:T(8,128)(2,1)S(1)}, bf16[32,80,256]{2,1,0:T(8,128)(2,1)}, u32[]{:S(2)}) copy-start(bf16[32,80,256]{2,1,0:T(8,128)(2,1)} %get-tuple-element.133) | copy-start | bytes 3932164
  1127.0 4.6 copy-start.34
  1127.0 4.7 copy-start.38
  1127.0 4.7 copy-start.39
  (16 other events, 33.3 us)
Sparse Core Ops, SparseCore 0:
  391.6 84.3 all-gather.4
  638.1 86.4 all-gather.2

commit v2 on v1

--- a/solution.py
+++ b/solution.py
@@ -712,6 +712,10 @@
             sum_ref[some, :] += from_above[step, z]
 
     rides = rides_of(planes, rides)
+    hurry = [-(-ride.count // steps) for ride in rides]
+    for ride, number in zip(rides, hurry):
+        for at in range(number):
+            ride.issue(jnp.int32(at))
     if product:
         factors = [
             pltpu.make_async_copy(operand, ref, factor_sems.at[i])
@@ -727,7 +731,6 @@
         start_loads(step)
 
     early = firsts + 1
-    hurry = [-(-ride.count // steps) for ride in rides]
 
     @pl.loop(0, steps + early + planes)
     def _(turn):
@@ -743,7 +746,7 @@
         stage(turn, add_core)
         for ride, number in zip(rides, hurry):
             for at in range(number):
-                ride.issue(turn * number + at)
+                ride.issue((turn + 1) * number + at)
         if whole_slice:
             stage(turn - 1, add_first)
         stage(turn - early + 1, add_second)

time: 1150 us -> 1130 us (0.983)
  Pallas kernels: 940 us -> 927 us
    pallas_call x7, Pallas kernels: 823 us -> 810 us  [communicate(): pl.pallas_call(kernel, out_shape=outputs + received, in_specs=[any_spec]...]
  transfers between devices with their start and end apart: 3 -> 3, of which waited for: 0 -> 0; matrix products, arithmetic and copies ran while one was open for 10% -> 11% of each run, Pallas kernels for 46% -> 45%
where the time goes in v2:
time: 1130 us
  Pallas kernels  927 us (82%)
  matrix products  110 us (10%)
  local copies, waits for them, and re-layouts  45.6 us (4%)
  other arithmetic  25.9 us (2%)
  between operations  15.2 us (1%)
    pallas_call x7, Pallas kernels, communicate(): pl.pallas_call(kernel, out_shape=outputs + received, in_specs=[any_spec]...  810 us
    pallas_call x2, Pallas kernels, orthogonalize(): pl.pallas_call(turn_kernel, grid=(pieces,), in_specs=[block] * 3, out_spe...  50.3 us
  transfers between devices with their start and end apart: 3, of which 0 were waited for; matrix products, arithmetic and copies ran while one was open for 11% of the time, Pallas kernels for 45%

profile of v2, /device:TPU:0, one launch (start us, length us, event | category | flops | bytes accessed | tf_op | source)
XLA Modules:
  0.0 1125.9 jit_solution(6975520827682769980)
XLA Ops:
  17.2 165.0 %gather_now.3 = (bf16[4,2,2,2,80,3072]{5,4,3,2,1,0:T(8,128)(2,1)}, bf16[4,2,2,2,16,128]{5,4,3,2,1,0:T(8,128)(2,1)}, bf16[4,2,2,2,80,2560]{5,4,3,2,1,0:T(8,128)(2,1)}, bf16[32,80,768]{2,1,0:T(8,128)(2,1)}) custom-call(bf16[80,3072]{1,0:T(8,128)(2,1)} %convert_element_type.79.refs_0_, bf16[16,128]{1,0:T(8,128)(2,1)} %pad.12.refs_1_, ...), custom_call_target="tpu_custom_call" | custom-call | bytes 209715200 | tf_op jit(solution)/shard_map/gather_now/pallas_call | solution.py:267
  185.6 7.9 convolution_convert_fusion.3.queries_ref
  195.1 35.4 %gather_now.4 = bf16[4,2,2,2,128,512]{5,4,3,2,1,0:T(8,128)(2,1)} custom-call(bf16[128,512]{1,0:T(8,128)(2,1)} %slice.86.refs_0_), custom_call_target="tpu_custom_call" | custom-call | bytes 209715200 | tf_op jit(solution)/shard_map/gather_now/pallas_call | solution.py:267
  232.4 11.4 %attend.1 = (bf16[128,2560]{1,0:T(8,128)(2,1)S(1)}, f32[5,256,128]{2,1,0:T(8,128)S(1)}) custom-call(s32[1]{0:T(128)} %bitcast.8.first_ref, bf16[128,3072]{1,0:T(8,128)(2,1)S(1)} %copy-done.11, bf16[2176,512]{1,0:T(8,128)(2,1)S(1)} %pad_dynamic-slice_fusion.kv_ref), custom_call_target="tpu_custom_call" | custom-call | flops 2852126720 | bytes 4194304 | tf_op jit(solution)/shard_map/attend/pallas_call | solution.py:1044
  243.9 10.3 multiply_reduce_fusion
  256.6 134.8 %gather_now.5 = (bf16[4,2,2,128,2560]{4,3,2,1,0:T(8,128)(2,1)}, bf16[4,2,2,128,2560]{4,3,2,1,0:T(8,128)(2,1)}, bf16[2560,768]{1,0:T(8,128)(2,1)}) custom-call(bf16[128,2560]{1,0:T(8,128)(2,1)} %multiply_convert_fusion.2.refs_0_, bf16[128,2560]{1,0:T(8,128)(2,1)} %refs_1_.1, bf16[2560,768]{1,0:T(8,128)(2,1)} %bitcast.79), custom_call_target="tpu_custom_call" | custom-call | bytes 209715200 | tf_op jit(solution)/shard_map/gather_now/pallas_call | solution.py:267
  402.3 6.8 attn_packets.1.refs_4_
  409.1 3.8 fusion.43
  416.7 13.2 %fusion.47 = f32[2048,1024]{1,0:T(8,128)} fusion(bf16[2048,2560]{1,0:T(8,128)(2,1)S(1)} %bitcast.98, bf16[2560,1024]{1,0:T(8,128)(2,1)S(1)} %maximum_select_fusion.refs_1_), kind=kOutput, calls=%fused_computation.92 | convolution fusion | flops 10737418240 | bytes 24117248 | tf_op jit(solution)/shard_map/dot_general | solution.py:1268
  429.9 14.7 %fusion.14 = (bf16[2048,512]{1,0:T(8,128)(2,1)S(1)}, bf16[2048,512]{1,0:T(8,128)(2,1)S(1)}, bf16[2048,512]{1,0:T(8,128)(2,1)S(1)}) fusion(f32[2048,1024]{1,0:T(8,128)} %fusion.47, bf16[2048,2560]{1,0:T(8,128)(2,1)} %bitcast.100, bf16[2560,512]{1,0:T(8,128)(2,1)S(1)} %maximum_select_fusion.1.refs_1_), kind=kOutput, calls=%fused_computation.24 | convolution fusion | flops 5395972096 | bytes 27787264 | tf_op jit(solution)/shard_map/dot_general | solution.py:1274
  448.6 7.0 convolution_convert_fusion.1
  455.6 5.9 convolution_convert_fusion
  463.8 164.5 %scatter_now.3 = (bf16[128,2560]{1,0:T(8,128)(2,1)}, bf16[2560,768]{1,0:T(8,128)(2,1)}, bf16[32,80,768]{2,1,0:T(8,128)(2,1)}, bf16[32,80,256]{2,1,0:T(8,128)(2,1)}, bf16[16,128,512]{2,1,0:T(8,128)(2,1)}) custom-call(bf16[4,2,2,128,1024]{4,3,2,1,0:T(8,128)(2,1)} %bitcast.78, bf16[2560,1024]{1,0:T(8,128)(2,1)} %copy-done.18, ...), custom_call_target="tpu_custom_call" | custom-call | bytes 209715200 | tf_op jit(solution)/shard_map/scatter_now/pallas_call | solution.py:267
  632.5 6.9 convolution_convert_fusion.2.grads_ref
  639.4 21.2 %attend_back.1 = (bf16[128,2560]{1,0:T(8,128)(2,1)S(1)}, bf16[2176,512]{1,0:T(8,128)(2,1)S(1)}) custom-call(s32[1]{0:T(128)} %bitcast.8.first_ref, bf16[128,3072]{1,0:T(8,128)(2,1)S(1)} %copy-done.12, bf16[128,2560]{1,0:T(8,128)(2,1)S(1)} %convolution_convert_fusion.2.grads_ref, f32[5,256,128]{2,1,0:T(8,128)S(1)} %copy-done.15, bf16[2176,512]{1,0:T(8,128)(2,1)} %copy-done.9), custom_call_target="tpu_custom_call" | custom-call | flops 7130316800 | bytes 8388608 | tf_op jit(solution)/shard_map/attend_back/pallas_call | solution.py:1116
  663.7 5.7 fusion.35
  669.4 9.3 fusion.15
  678.7 3.8 pad_maximum_fusion.grads_ref
  682.6 37.3 %orthogonalize.2 = (bf16[2560,768]{1,0:T(8,128)(2,1)S(1)}, bf16[2560,768]{1,0:T(8,128)(2,1)}) custom-call(f32[2560,768]{1,0:T(8,128)} %pad_maximum_fusion.grads_ref, bf16[2560,768]{1,0:T(8,128)(2,1)} %get-tuple-element.114.others_ref, bf16[2560,768]{1,0:T(8,128)(2,1)} %bitcast.103), custom_call_target="tpu_custom_call" | custom-call | flops 10066329600 | bytes 23592960 | tf_op jit(solution)/shard_map/orthogonalize/pallas_call | solution.py:914
  721.7 111.7 %scatter_now.4 = (bf16[128,512]{1,0:T(8,128)(2,1)}, bf16[32,80,768]{2,1,0:T(8,128)(2,1)}) custom-call(bf16[4,2,2,2,128,512]{5,4,3,2,1,0:T(8,128)(2,1)} %bitcast.76, bf16[32,80,768]{2,1,0:T(8,128)(2,1)} %bitcast.69), custom_call_target="tpu_custom_call" | custom-call | bytes 209715200 | tf_op jit(solution)/shard_map/scatter_now/pallas_call | solution.py:267
  837.9 146.6 %scatter_now.5 = (bf16[128,2560]{1,0:T(8,128)(2,1)}, bf16[32,80,768]{2,1,0:T(8,128)(2,1)}, bf16[16,128,512]{2,1,0:T(8,128)(2,1)}) custom-call(bf16[4,2,2,128,512]{4,3,2,1,0:T(8,128)(2,1)} %bitcast.89, bf16[2560,512]{1,0:T(8,128)(2,1)} %copy-done.22, bf16[32,80,768]{2,1,0:T(8,128)(2,1)} %bitcast.81, bf16[6,128,512]{2,1,0:T(8,128)(2,1)} %bitcast.85), custom_call_target="tpu_custom_call" | custom-call | bytes 209715200 | tf_op jit(solution)/shard_map/scatter_now/pallas_call | solution.py:267
  984.6 8.3 conditional.7
  984.6 8.3 convolution_bitcast_fusion.1
  996.8 12.2 %fusion.27 = (f32[2560]{0:T(1024)S(1)}, f32[128]{0:T(128)S(1)}, f32[128,2560]{1,0:T(8,128)}) fusion(bf16[128,2560]{1,0:T(8,128)(2,1)S(1)} %copy-done.21, f32[128]{0:T(128)S(1)} %copy-done.36, f32[2560]{0:T(1024)S(1)} %copy-done.33, bf16[128,3072]{1,0:T(8,128)(2,1)} %copy-done.23, bf16[2560,3072]{1,0:T(8,128)(2,1)} %bitcast.73), kind=kOutput, calls=%fused_computation.55 | convolution fusion | flops 2015556992 | bytes 18502656 | tf_op jit(solution)/shard_map/tc,dc->td/dot_general | solution.py:1327
  1011.6 15.9 %ffn_update.1 = (f32[2,80,7680]{2,1,0:T(8,128)}, f32[2,80,7680]{2,1,0:T(8,128)}, bf16[2,80,7680]{2,1,0:T(8,128)(2,1)}, f32[80,7680]{1,0:T(8,128)}, f32[80,7680]{1,0:T(8,128)}, /*index=5*/bf16[80,7680]{1,0:T(8,128)(2,1)}) custom-call(bf16[32,80,768]{2,1,0:T(8,128)(2,1)} %get-tuple-element.129.grad_ref, bf16[32,80,768]{2,1,0:T(8,128)(2,1)} %get-tuple-element.130.turn_ref, ...), custom_call_target="tpu_custom_call" | custom-call | bytes 52428800 | tf_op jit(solution)/shard_map/ffn_update/pallas_call | solution.py:964
  1029.8 12.3 %conditional.8 = (f32[2560,256]{1,0:T(8,128)}) conditional(s32[]{:T(128)} %convert_element_type.93, (bf16[16,128,512]{2,1,0:T(8,128)(2,1)}, s32[]{:T(128)}, bf16[2048,2560]{1,0:T(8,128)(2,1)}) %tuple.37, (bf16[16,128,512]{2,1,0:T(8,128)(2,1)}, s32[]{:T(128)}, bf16[2048,2560]{1,0:T(8,128)(2,1)}) %tuple.38), branch_computations={%region_6.7_spmd, %region_7.8_spmd} | conditional | flops 2684354560 | bytes 19398714 | solution.py:1352
  1029.8 8.8 convolution_bitcast_fusion.3
  1038.6 3.2 copy.55
  1042.1 13.1 %orthogonalize.3 = bf16[2560,512]{1,0:T(8,128)(2,1)S(1)} custom-call(f32[2560,256]{1,0:T(8,128)} %get-tuple-element.147.grads_ref, bf16[2560,256]{1,0:T(8,128)(2,1)} %collective-permute-done.others_ref, bf16[2560,256]{1,0:T(8,128)(2,1)S(1)} %bitcast.71), custom_call_target="tpu_custom_call" | custom-call | flops 3355443200 | bytes 7864320 | tf_op jit(solution)/shard_map/orthogonalize/pallas_call | solution.py:914
  1056.7 51.5 %exchange_now.1 = (bf16[32,80,512]{2,1,0:T(8,128)(2,1)}, f32[32,8,128]{2,1,0:T(8,128)}) custom-call(bf16[32,80,512]{2,1,0:T(8,128)(2,1)} %bitcast.70, f32[32,8,128]{2,1,0:T(8,128)} %pad.14.refs_1_), custom_call_target="tpu_custom_call" | custom-call | bytes 104857600 | tf_op jit(solution)/shard_map/exchange_now/pallas_call | solution.py:267
  1108.2 5.1 attn_update.2
  1113.3 4.6 attn_update.3
  (143 shorter events, 64.2 us)
Async XLA Ops:
  7.2 4.2 copy-start.37
  7.2 4.2 copy-start.4
  7.2 977.3 %all-gather.5.cloned.1.call-start = ((), (), s32[]{:S(2)}) async-start(), calls=%async_computation.1 | async-start | bytes 11141120 | tf_op jit(solution)/shard_map/all_gather | solution.py:1228
  16.6 166.7 %copy-start.19 = (bf16[128,2560]{1,0:T(8,128)(2,1)S(1)}, bf16[128,2560]{1,0:T(8,128)(2,1)}, u32[]{:S(2)}) copy-start(bf16[128,2560]{1,0:T(8,128)(2,1)} %param.16) | copy-start | bytes 1966084
  183.3 10.2 copy-start.32
  232.4 11.5 %copy-start.9 = (bf16[2176,512]{1,0:T(8,128)(2,1)}, bf16[2176,512]{1,0:T(8,128)(2,1)S(1)}, u32[]{:S(2)}) copy-start(bf16[2176,512]{1,0:T(8,128)(2,1)S(1)} %pad_dynamic-slice_fusion.kv_ref) | copy-start | bytes 6684676
  232.4 11.5 %copy-start.20 = (bf16[128,2560]{1,0:T(8,128)(2,1)S(1)}, bf16[128,2560]{1,0:T(8,128)(2,1)}, u32[]{:S(2)}) copy-start(bf16[128,2560]{1,0:T(8,128)(2,1)} %param.16) | copy-start | bytes 1966084
  243.9 10.4 copy-start.14
  391.5 593.1 %all-gather.3.cloned.1.call-start = ((), (), s32[]{:S(2)}) async-start(), calls=%async_computation | async-start | bytes 11141120 | tf_op jit(solution)/shard_map/all_gather | solution.py:1228
  409.1 5.6 slice-start
  409.1 6.9 slice-start.1
  413.4 16.5 %copy-start.22 = (bf16[2560,512]{1,0:T(8,128)(2,1)}, bf16[2560,512]{1,0:T(8,128)(2,1)S(1)}, u32[]{:S(2)}) copy-start(bf16[2560,512]{1,0:T(8,128)(2,1)S(1)} %maximum_select_fusion.1.refs_1_) | copy-start | bytes 7864324
  416.7 13.2 %copy-start.18 = (bf16[2560,1024]{1,0:T(8,128)(2,1)}, bf16[2560,1024]{1,0:T(8,128)(2,1)S(1)}, u32[]{:S(2)}) copy-start(bf16[2560,1024]{1,0:T(8,128)(2,1)S(1)} %maximum_select_fusion.refs_1_) | copy-start | bytes 15728644
  444.6 4.0 copy-start.28
  463.7 164.6 %copy-start.16 = (f32[128,2560]{1,0:T(8,128)S(1)}, f32[128,2560]{1,0:T(8,128)}, u32[]{:S(2)}) copy-start(f32[128,2560]{1,0:T(8,128)} %get-tuple-element.173) | copy-start | bytes 3932164
  463.8 166.2 %copy-start.24 = (bf16[128,2560]{1,0:T(8,128)(2,1)S(1)}, bf16[128,2560]{1,0:T(8,128)(2,1)}, u32[]{:S(2)}) copy-start(bf16[128,2560]{1,0:T(8,128)(2,1)} %refs_1_.1) | copy-start | bytes 1966084
  632.4 6.9 copy-start.12
  632.4 6.9 copy-start.15
  663.7 5.8 copy-start.30
  834.4 150.1 %copy-start.23 = (bf16[128,3072]{1,0:T(8,128)(2,1)}, bf16[128,3072]{1,0:T(8,128)(2,1)S(1)}, u32[]{:S(2)}) copy-start(bf16[128,3072]{1,0:T(8,128)(2,1)S(1)} %constant_dynamic-update-slice_fusion) | copy-start | bytes 2359300
  992.9 3.9 copy-start.36
  995.5 46.6 %collective-permute-start = (bf16[2560,256]{1,0:T(8,128)(2,1)}, bf16[2560,256]{1,0:T(8,128)(2,1)}, u32[]{:S(2)}, u32[]{:S(2)}) collective-permute-start(bf16[2560,256]{1,0:T(8,128)(2,1)} %copy.47), channel_id=1, source_target_pairs={{0,1},{1,0},{2,3},{3,2},{4,5},{5,4},{6,7},{7,6},{8,9},{9,8},{10,11... | collective-permute-start | bytes 3932168 | tf_op jit(solution)/shard_map/ppermute | solution.py:1189
  1011.6 15.9 %copy-start.41 = (f32[128]{0:T(128)S(1)}, f32[128]{0:T(128)}, u32[]{:S(2)}) copy-start(f32[128]{0:T(128)} %copy-done.40) | copy-start | bytes 1540
  1011.6 15.9 %copy-start.17 = (f32[128,2560]{1,0:T(8,128)S(1)}, f32[128,2560]{1,0:T(8,128)}, u32[]{:S(2)}) copy-start(f32[128,2560]{1,0:T(8,128)} %get-tuple-element.173) | copy-start | bytes 3932164
  1011.6 16.0 %copy-start.25 = (bf16[128,2560]{1,0:T(8,128)(2,1)S(1)}, bf16[128,2560]{1,0:T(8,128)(2,1)}, u32[]{:S(2)}) copy-start(bf16[128,2560]{1,0:T(8,128)(2,1)} %refs_1_.1) | copy-start | bytes 1966084
  1011.6 16.0 %copy-start.26 = (bf16[128,2560]{1,0:T(8,128)(2,1)S(1)}, bf16[128,2560]{1,0:T(8,128)(2,1)}, u32[]{:S(2)}) copy-start(bf16[128,2560]{1,0:T(8,128)(2,1)} %get-tuple-element.117) | copy-start | bytes 1966084
  1011.6 16.0 %copy-start.27 = (f32[128,2560]{1,0:T(8,128)S(1)}, f32[128,2560]{1,0:T(8,128)}, u32[]{:S(2)}) copy-start(f32[128,2560]{1,0:T(8,128)} %get-tuple-element.174) | copy-start | bytes 3932164
  1011.6 16.0 %copy-start.31 = (bf16[128,2560]{1,0:T(8,128)(2,1)S(1)}, bf16[128,2560]{1,0:T(8,128)(2,1)}, u32[]{:S(2)}) copy-start(bf16[128,2560]{1,0:T(8,128)(2,1)} %get-tuple-element.123) | copy-start | bytes 1966084
  1029.8 12.3 %copy-start.13 = (bf16[32,80,256]{2,1,0:T(8,128)(2,1)S(1)}, bf16[32,80,256]{2,1,0:T(8,128)(2,1)}, u32[]{:S(2)}) copy-start(bf16[32,80,256]{2,1,0:T(8,128)(2,1)} %get-tuple-element.133) | copy-start | bytes 3932164
  1113.3 4.6 copy-start.34
  1113.3 4.7 copy-start.38
  1113.3 4.7 copy-start.39
  (16 other events, 32.9 us)
Sparse Core Ops, SparseCore 0:
  391.6 92.9 all-gather.4
  632.5 87.1 all-gather.2

commit v3 on v2

--- a/solution.py
+++ b/solution.py
@@ -714,7 +714,7 @@
     rides = rides_of(planes, rides)
     hurry = [-(-ride.count // steps) for ride in rides]
     for ride, number in zip(rides, hurry):
-        for at in range(number):
+        for at in range(2 * number):
             ride.issue(jnp.int32(at))
     if product:
         factors = [
@@ -746,7 +746,7 @@
         stage(turn, add_core)
         for ride, number in zip(rides, hurry):
             for at in range(number):
-                ride.issue((turn + 1) * number + at)
+                ride.issue((turn + 2) * number + at)
         if whole_slice:
             stage(turn - 1, add_first)
         stage(turn - early + 1, add_second)

time: 1130 us -> 1150 us (1.018)
  Pallas kernels: 927 us -> 942 us
    pallas_call x7, Pallas kernels: 810 us -> 825 us  [communicate(): pl.pallas_call(kernel, out_shape=outputs + received, in_specs=[any_spec]...]
  transfers between devices with their start and end apart: 3 -> 3, of which waited for: 0 -> 0; matrix products, arithmetic and copies ran while one was open for 11% -> 10% of each run, Pallas kernels for 45% -> 45%
where the time goes in v3:
time: 1150 us; the launch traced here: 1140 us
  Pallas kernels  942 us (82%)
  matrix products  110 us (10%)
  local copies, waits for them, and re-layouts  45.6 us (4%)
  other arithmetic  25.9 us (2%)
  between operations  15.2 us (1%)
    pallas_call x7, Pallas kernels, communicate(): pl.pallas_call(kernel, out_shape=outputs + received, in_specs=[any_spec]...  825 us
    pallas_call x2, Pallas kernels, orthogonalize(): pl.pallas_call(turn_kernel, grid=(pieces,), in_specs=[block] * 3, out_spe...  50.3 us
  transfers between devices with their start and end apart: 3, of which 0 were waited for; matrix products, arithmetic and copies ran while one was open for 10% of the time, Pallas kernels for 45%

profile of v3, /device:TPU:0, one launch (start us, length us, event | category | flops | bytes accessed | tf_op | source)
XLA Modules:
  0.0 1139.9 jit_solution(14897414655073592879)
XLA Ops:
  17.2 165.0 %gather_now.3 = (bf16[4,2,2,2,80,3072]{5,4,3,2,1,0:T(8,128)(2,1)}, bf16[4,2,2,2,16,128]{5,4,3,2,1,0:T(8,128)(2,1)}, bf16[4,2,2,2,80,2560]{5,4,3,2,1,0:T(8,128)(2,1)}, bf16[32,80,768]{2,1,0:T(8,128)(2,1)}) custom-call(bf16[80,3072]{1,0:T(8,128)(2,1)} %convert_element_type.79.refs_0_, bf16[16,128]{1,0:T(8,128)(2,1)} %pad.12.refs_1_, ...), custom_call_target="tpu_custom_call" | custom-call | bytes 209715200 | tf_op jit(solution)/shard_map/gather_now/pallas_call | solution.py:267
  185.6 7.9 convolution_convert_fusion.3.queries_ref
  195.1 35.4 %gather_now.4 = bf16[4,2,2,2,128,512]{5,4,3,2,1,0:T(8,128)(2,1)} custom-call(bf16[128,512]{1,0:T(8,128)(2,1)} %slice.86.refs_0_), custom_call_target="tpu_custom_call" | custom-call | bytes 209715200 | tf_op jit(solution)/shard_map/gather_now/pallas_call | solution.py:267
  232.4 11.4 %attend.1 = (bf16[128,2560]{1,0:T(8,128)(2,1)S(1)}, f32[5,256,128]{2,1,0:T(8,128)S(1)}) custom-call(s32[1]{0:T(128)} %bitcast.8.first_ref, bf16[128,3072]{1,0:T(8,128)(2,1)S(1)} %copy-done.11, bf16[2176,512]{1,0:T(8,128)(2,1)S(1)} %pad_dynamic-slice_fusion.kv_ref), custom_call_target="tpu_custom_call" | custom-call | flops 2852126720 | bytes 4194304 | tf_op jit(solution)/shard_map/attend/pallas_call | solution.py:1044
  243.9 10.3 multiply_reduce_fusion
  256.6 134.8 %gather_now.5 = (bf16[4,2,2,128,2560]{4,3,2,1,0:T(8,128)(2,1)}, bf16[4,2,2,128,2560]{4,3,2,1,0:T(8,128)(2,1)}, bf16[2560,768]{1,0:T(8,128)(2,1)}) custom-call(bf16[128,2560]{1,0:T(8,128)(2,1)} %multiply_convert_fusion.2.refs_0_, bf16[128,2560]{1,0:T(8,128)(2,1)} %refs_1_.1, bf16[2560,768]{1,0:T(8,128)(2,1)} %bitcast.79), custom_call_target="tpu_custom_call" | custom-call | bytes 209715200 | tf_op jit(solution)/shard_map/gather_now/pallas_call | solution.py:267
  402.3 6.8 attn_packets.1.refs_4_
  409.1 3.8 fusion.43
  416.7 13.2 %fusion.47 = f32[2048,1024]{1,0:T(8,128)} fusion(bf16[2048,2560]{1,0:T(8,128)(2,1)S(1)} %bitcast.98, bf16[2560,1024]{1,0:T(8,128)(2,1)S(1)} %maximum_select_fusion.refs_1_), kind=kOutput, calls=%fused_computation.92 | convolution fusion | flops 10737418240 | bytes 24117248 | tf_op jit(solution)/shard_map/dot_general | solution.py:1268
  429.9 14.7 %fusion.14 = (bf16[2048,512]{1,0:T(8,128)(2,1)S(1)}, bf16[2048,512]{1,0:T(8,128)(2,1)S(1)}, bf16[2048,512]{1,0:T(8,128)(2,1)S(1)}) fusion(f32[2048,1024]{1,0:T(8,128)} %fusion.47, bf16[2048,2560]{1,0:T(8,128)(2,1)} %bitcast.100, bf16[2560,512]{1,0:T(8,128)(2,1)S(1)} %maximum_select_fusion.1.refs_1_), kind=kOutput, calls=%fused_computation.24 | convolution fusion | flops 5395972096 | bytes 27787264 | tf_op jit(solution)/shard_map/dot_general | solution.py:1274
  448.6 7.0 convolution_convert_fusion.1
  455.6 5.9 convolution_convert_fusion
  463.8 169.8 %scatter_now.3 = (bf16[128,2560]{1,0:T(8,128)(2,1)}, bf16[2560,768]{1,0:T(8,128)(2,1)}, bf16[32,80,768]{2,1,0:T(8,128)(2,1)}, bf16[32,80,256]{2,1,0:T(8,128)(2,1)}, bf16[16,128,512]{2,1,0:T(8,128)(2,1)}) custom-call(bf16[4,2,2,128,1024]{4,3,2,1,0:T(8,128)(2,1)} %bitcast.78, bf16[2560,1024]{1,0:T(8,128)(2,1)} %copy-done.18, ...), custom_call_target="tpu_custom_call" | custom-call | bytes 209715200 | tf_op jit(solution)/shard_map/scatter_now/pallas_call | solution.py:267
  637.7 6.9 convolution_convert_fusion.2.grads_ref
  644.6 21.3 %attend_back.1 = (bf16[128,2560]{1,0:T(8,128)(2,1)S(1)}, bf16[2176,512]{1,0:T(8,128)(2,1)S(1)}) custom-call(s32[1]{0:T(128)} %bitcast.8.first_ref, bf16[128,3072]{1,0:T(8,128)(2,1)S(1)} %copy-done.12, bf16[128,2560]{1,0:T(8,128)(2,1)S(1)} %convolution_convert_fusion.2.grads_ref, f32[5,256,128]{2,1,0:T(8,128)S(1)} %copy-done.15, bf16[2176,512]{1,0:T(8,128)(2,1)} %copy-done.9), custom_call_target="tpu_custom_call" | custom-call | flops 7130316800 | bytes 8388608 | tf_op jit(solution)/shard_map/attend_back/pallas_call | solution.py:1116
  669.0 5.7 fusion.35
  674.8 8.7 fusion.15
  683.5 3.8 pad_maximum_fusion.grads_ref
  687.3 37.3 %orthogonalize.2 = (bf16[2560,768]{1,0:T(8,128)(2,1)S(1)}, bf16[2560,768]{1,0:T(8,128)(2,1)}) custom-call(f32[2560,768]{1,0:T(8,128)} %pad_maximum_fusion.grads_ref, bf16[2560,768]{1,0:T(8,128)(2,1)} %get-tuple-element.114.others_ref, bf16[2560,768]{1,0:T(8,128)(2,1)} %bitcast.103), custom_call_target="tpu_custom_call" | custom-call | flops 10066329600 | bytes 23592960 | tf_op jit(solution)/shard_map/orthogonalize/pallas_call | solution.py:914
  726.5 114.6 %scatter_now.4 = (bf16[128,512]{1,0:T(8,128)(2,1)}, bf16[32,80,768]{2,1,0:T(8,128)(2,1)}) custom-call(bf16[4,2,2,2,128,512]{5,4,3,2,1,0:T(8,128)(2,1)} %bitcast.76, bf16[32,80,768]{2,1,0:T(8,128)(2,1)} %bitcast.69), custom_call_target="tpu_custom_call" | custom-call | bytes 209715200 | tf_op jit(solution)/shard_map/scatter_now/pallas_call | solution.py:267
  845.5 149.0 %scatter_now.5 = (bf16[128,2560]{1,0:T(8,128)(2,1)}, bf16[32,80,768]{2,1,0:T(8,128)(2,1)}, bf16[16,128,512]{2,1,0:T(8,128)(2,1)}) custom-call(bf16[4,2,2,128,512]{4,3,2,1,0:T(8,128)(2,1)} %bitcast.89, bf16[2560,512]{1,0:T(8,128)(2,1)} %copy-done.22, bf16[32,80,768]{2,1,0:T(8,128)(2,1)} %bitcast.81, bf16[6,128,512]{2,1,0:T(8,128)(2,1)} %bitcast.85), custom_call_target="tpu_custom_call" | custom-call | bytes 209715200 | tf_op jit(solution)/shard_map/scatter_now/pallas_call | solution.py:267
  994.6 8.3 conditional.7
  994.6 8.3 convolution_bitcast_fusion.1
  1006.2 12.2 %fusion.27 = (f32[2560]{0:T(1024)S(1)}, f32[128]{0:T(128)S(1)}, f32[128,2560]{1,0:T(8,128)}) fusion(bf16[128,2560]{1,0:T(8,128)(2,1)S(1)} %copy-done.21, f32[128]{0:T(128)S(1)} %copy-done.36, f32[2560]{0:T(1024)S(1)} %copy-done.33, bf16[128,3072]{1,0:T(8,128)(2,1)} %copy-done.23, bf16[2560,3072]{1,0:T(8,128)(2,1)} %bitcast.73), kind=kOutput, calls=%fused_computation.55 | convolution fusion | flops 2015556992 | bytes 18502656 | tf_op jit(solution)/shard_map/tc,dc->td/dot_general | solution.py:1327
  1021.0 15.9 %ffn_update.1 = (f32[2,80,7680]{2,1,0:T(8,128)}, f32[2,80,7680]{2,1,0:T(8,128)}, bf16[2,80,7680]{2,1,0:T(8,128)(2,1)}, f32[80,7680]{1,0:T(8,128)}, f32[80,7680]{1,0:T(8,128)}, /*index=5*/bf16[80,7680]{1,0:T(8,128)(2,1)}) custom-call(bf16[32,80,768]{2,1,0:T(8,128)(2,1)} %get-tuple-element.129.grad_ref, bf16[32,80,768]{2,1,0:T(8,128)(2,1)} %get-tuple-element.130.turn_ref, ...), custom_call_target="tpu_custom_call" | custom-call | bytes 52428800 | tf_op jit(solution)/shard_map/ffn_update/pallas_call | solution.py:964
  1039.2 12.3 %conditional.8 = (f32[2560,256]{1,0:T(8,128)}) conditional(s32[]{:T(128)} %convert_element_type.93, (bf16[16,128,512]{2,1,0:T(8,128)(2,1)}, s32[]{:T(128)}, bf16[2048,2560]{1,0:T(8,128)(2,1)}) %tuple.37, (bf16[16,128,512]{2,1,0:T(8,128)(2,1)}, s32[]{:T(128)}, bf16[2048,2560]{1,0:T(8,128)(2,1)}) %tuple.38), branch_computations={%region_6.7_spmd, %region_7.8_spmd} | conditional | flops 2684354560 | bytes 19398714 | solution.py:1352
  1039.2 8.8 convolution_bitcast_fusion.3
  1048.0 3.2 copy.55
  1051.5 13.1 %orthogonalize.3 = bf16[2560,512]{1,0:T(8,128)(2,1)S(1)} custom-call(f32[2560,256]{1,0:T(8,128)} %get-tuple-element.147.grads_ref, bf16[2560,256]{1,0:T(8,128)(2,1)} %collective-permute-done.others_ref, bf16[2560,256]{1,0:T(8,128)(2,1)S(1)} %bitcast.71), custom_call_target="tpu_custom_call" | custom-call | flops 3355443200 | bytes 7864320 | tf_op jit(solution)/shard_map/orthogonalize/pallas_call | solution.py:914
  1066.1 56.1 %exchange_now.1 = (bf16[32,80,512]{2,1,0:T(8,128)(2,1)}, f32[32,8,128]{2,1,0:T(8,128)}) custom-call(bf16[32,80,512]{2,1,0:T(8,128)(2,1)} %bitcast.70, f32[32,8,128]{2,1,0:T(8,128)} %pad.14.refs_1_), custom_call_target="tpu_custom_call" | custom-call | bytes 104857600 | tf_op jit(solution)/shard_map/exchange_now/pallas_call | solution.py:267
  1122.2 5.1 attn_update.2
  1127.4 4.6 attn_update.3
  (143 shorter events, 63.6 us)
Async XLA Ops:
  7.2 4.2 copy-start.37
  7.2 4.2 copy-start.4
  7.2 987.3 %all-gather.5.cloned.1.call-start = ((), (), s32[]{:S(2)}) async-start(), calls=%async_computation.1 | async-start | bytes 11141120 | tf_op jit(solution)/shard_map/all_gather | solution.py:1228
  16.6 166.7 %copy-start.19 = (bf16[128,2560]{1,0:T(8,128)(2,1)S(1)}, bf16[128,2560]{1,0:T(8,128)(2,1)}, u32[]{:S(2)}) copy-start(bf16[128,2560]{1,0:T(8,128)(2,1)} %param.16) | copy-start | bytes 1966084
  183.3 10.2 copy-start.32
  232.4 11.5 %copy-start.9 = (bf16[2176,512]{1,0:T(8,128)(2,1)}, bf16[2176,512]{1,0:T(8,128)(2,1)S(1)}, u32[]{:S(2)}) copy-start(bf16[2176,512]{1,0:T(8,128)(2,1)S(1)} %pad_dynamic-slice_fusion.kv_ref) | copy-start | bytes 6684676
  232.4 11.5 %copy-start.20 = (bf16[128,2560]{1,0:T(8,128)(2,1)S(1)}, bf16[128,2560]{1,0:T(8,128)(2,1)}, u32[]{:S(2)}) copy-start(bf16[128,2560]{1,0:T(8,128)(2,1)} %param.16) | copy-start | bytes 1966084
  243.9 10.4 copy-start.14
  391.5 603.1 %all-gather.3.cloned.1.call-start = ((), (), s32[]{:S(2)}) async-start(), calls=%async_computation | async-start | bytes 11141120 | tf_op jit(solution)/shard_map/all_gather | solution.py:1228
  409.1 5.6 slice-start
  409.1 6.9 slice-start.1
  413.4 16.5 %copy-start.22 = (bf16[2560,512]{1,0:T(8,128)(2,1)}, bf16[2560,512]{1,0:T(8,128)(2,1)S(1)}, u32[]{:S(2)}) copy-start(bf16[2560,512]{1,0:T(8,128)(2,1)S(1)} %maximum_select_fusion.1.refs_1_) | copy-start | bytes 7864324
  416.7 13.2 %copy-start.18 = (bf16[2560,1024]{1,0:T(8,128)(2,1)}, bf16[2560,1024]{1,0:T(8,128)(2,1)S(1)}, u32[]{:S(2)}) copy-start(bf16[2560,1024]{1,0:T(8,128)(2,1)S(1)} %maximum_select_fusion.refs_1_) | copy-start | bytes 15728644
  444.6 4.0 copy-start.28
  463.7 169.8 %copy-start.16 = (f32[128,2560]{1,0:T(8,128)S(1)}, f32[128,2560]{1,0:T(8,128)}, u32[]{:S(2)}) copy-start(f32[128,2560]{1,0:T(8,128)} %get-tuple-element.173) | copy-start | bytes 3932164
  463.8 171.5 %copy-start.24 = (bf16[128,2560]{1,0:T(8,128)(2,1)S(1)}, bf16[128,2560]{1,0:T(8,128)(2,1)}, u32[]{:S(2)}) copy-start(bf16[128,2560]{1,0:T(8,128)(2,1)} %refs_1_.1) | copy-start | bytes 1966084
  637.7 6.9 copy-start.12
  637.7 6.9 copy-start.15
  669.0 5.8 copy-start.30
  842.0 152.5 %copy-start.23 = (bf16[128,3072]{1,0:T(8,128)(2,1)}, bf16[128,3072]{1,0:T(8,128)(2,1)S(1)}, u32[]{:S(2)}) copy-start(bf16[128,3072]{1,0:T(8,128)(2,1)S(1)} %constant_dynamic-update-slice_fusion) | copy-start | bytes 2359300
  1002.9 3.3 copy-start.36
  1005.6 46.0 %collective-permute-start = (bf16[2560,256]{1,0:T(8,128)(2,1)}, bf16[2560,256]{1,0:T(8,128)(2,1)}, u32[]{:S(2)}, u32[]{:S(2)}) collective-permute-start(bf16[2560,256]{1,0:T(8,128)(2,1)} %copy.47), channel_id=1, source_target_pairs={{0,1},{1,0},{2,3},{3,2},{4,5},{5,4},{6,7},{7,6},{8,9},{9,8},{10,11... | collective-permute-start | bytes 3932168 | tf_op jit(solution)/shard_map/ppermute | solution.py:1189
  1021.0 15.9 %copy-start.41 = (f32[128]{0:T(128)S(1)}, f32[128]{0:T(128)}, u32[]{:S(2)}) copy-start(f32[128]{0:T(128)} %copy-done.40) | copy-start | bytes 1540
  1021.0 15.9 %copy-start.17 = (f32[128,2560]{1,0:T(8,128)S(1)}, f32[128,2560]{1,0:T(8,128)}, u32[]{:S(2)}) copy-start(f32[128,2560]{1,0:T(8,128)} %get-tuple-element.173) | copy-start | bytes 3932164
  1021.0 16.0 %copy-start.25 = (bf16[128,2560]{1,0:T(8,128)(2,1)S(1)}, bf16[128,2560]{1,0:T(8,128)(2,1)}, u32[]{:S(2)}) copy-start(bf16[128,2560]{1,0:T(8,128)(2,1)} %refs_1_.1) | copy-start | bytes 1966084
  1021.0 16.0 %copy-start.26 = (bf16[128,2560]{1,0:T(8,128)(2,1)S(1)}, bf16[128,2560]{1,0:T(8,128)(2,1)}, u32[]{:S(2)}) copy-start(bf16[128,2560]{1,0:T(8,128)(2,1)} %get-tuple-element.117) | copy-start | bytes 1966084
  1021.0 16.0 %copy-start.27 = (f32[128,2560]{1,0:T(8,128)S(1)}, f32[128,2560]{1,0:T(8,128)}, u32[]{:S(2)}) copy-start(f32[128,2560]{1,0:T(8,128)} %get-tuple-element.174) | copy-start | bytes 3932164
  1021.0 16.0 %copy-start.31 = (bf16[128,2560]{1,0:T(8,128)(2,1)S(1)}, bf16[128,2560]{1,0:T(8,128)(2,1)}, u32[]{:S(2)}) copy-start(bf16[128,2560]{1,0:T(8,128)(2,1)} %get-tuple-element.123) | copy-start | bytes 1966084
  1039.2 12.3 %copy-start.13 = (bf16[32,80,256]{2,1,0:T(8,128)(2,1)S(1)}, bf16[32,80,256]{2,1,0:T(8,128)(2,1)}, u32[]{:S(2)}) copy-start(bf16[32,80,256]{2,1,0:T(8,128)(2,1)} %get-tuple-element.133) | copy-start | bytes 3932164
  1127.3 4.6 copy-start.34
  1127.4 4.7 copy-start.38
  1127.4 4.7 copy-start.39
  (16 other events, 31.7 us)
Sparse Core Ops, SparseCore 0:
  391.6 92.9 all-gather.4
  637.8 86.8 all-gather.2
